TPU v7x, 32 devices: a whole 2x2x4 slice. The times are simulated.
32 devices in a mesh: sr: 4 (over y, x), az: 8 (over z, core).
Axes of the slice: x: 2, y: 2, z: 4, core: 2. Of those that a mesh axis runs over, the one named last changes fastest.
Arguments:
- residual: float32 [16, 128, 10, 128], P('sr', 'az'), may hold values from -6 to 6
- dinv: float32 [16, 128, 10, 10, 128], P('sr', 'az')
- wall_jac: float32 [16, 128, 10, 10], P('sr', 'az'), may hold values from -2 to 2
- lower_coef: float32 [16, 128, 128], P('sr', 'az'), may hold values from 0.2 to 0.6
- upper_coef: float32 [16, 128, 128], P('sr', 'az'), may hold values from 0.2 to 0.6
- off_jac: float32 [4, 16, 128, 10, 10], P(None, 'sr', 'az'), may hold values from -0.7 to 0.7
- lengths: int32 [16, 128], P('sr', 'az'), may hold values from 32 to 128, as said below
- axis_flag: int32 [128], P('az'), may hold values 0 or 1
- partner: int32 [128], P('az'), may hold values from 0 to 15, as said below
Outputs:
- update: float32 [16, 128, 10, 128], P('sr', 'az')
- next_rhs: float32 [16, 128, 10, 128], P('sr', 'az')
Inputs may be any that keep to these rules, and one draw needn't show every extreme that they name: `lengths`: active points of a line; some line has all 128. `partner`: within each aligned block of 16 azimuths the entries are a permutation of 0 to 15.
All inputs are finite; a program needn't handle non-finite values. No bound on the sum of `axis_flag` on one device may be relied on, other than what follows from the above.
Results may differ from a plain program's by a relative error of at most 0.0001.
Values sent between devices are 32-bit elements; how exact they have to be, the bound alone decides.
A program may use at most 64 MiB of HBM per device.

v0:
```python
import jax
import jax.numpy as jnp
from jax import lax
from jax.sharding import PartitionSpec as P

INNER = 4
SWEEPS = 2


HIGH = lax.Precision.HIGHEST


def from_behind(value, axis, by):
    size = lax.axis_size(axis)
    return lax.ppermute(value, axis, [(i, (i + by) % size) for i in range(size)])


def with_halo(block, sides, width, periodic):
    for axis, dim in sides:
        count = lax.axis_size(axis)
        forward = [(i, i + 1) for i in range(count - 1)]
        if periodic:
            forward.append((count - 1, 0))
        backward = [(target, source) for source, target in forward]
        low = lax.ppermute(
            lax.slice_in_dim(block, block.shape[dim] - width, None, axis=dim), axis, forward
        )
        high = lax.ppermute(lax.slice_in_dim(block, 0, width, axis=dim), axis, backward)
        block = jnp.concatenate([low, block, high], axis=dim)
    return block


def solve_lines(rhs, dinv, wall_jac, lower_coef, upper_coef, active):

    def apply_inverse(vec):
        return jnp.einsum("...abw,...bw->...aw", dinv, vec, precision=HIGH)

    mask = active[..., None, :]
    update = apply_inverse(rhs) * mask
    for step in range(INNER):
        zeros = jnp.zeros_like(update[..., :1])
        below = jnp.concatenate([zeros, update[..., :-1]], axis=-1)
        above = jnp.concatenate([update[..., 1:], zeros], axis=-1)
        cross = lower_coef[..., None, :] * jnp.einsum(
            "...ab,...bw->...aw", wall_jac, below, precision=HIGH
        )
        cross = cross + upper_coef[..., None, :] * jnp.einsum(
            "...ba,...bw->...aw", wall_jac, above, precision=HIGH
        )
        update = apply_inverse(rhs - cross) * mask
    return update


def neighbour_sum(update, off_jac, axis_flag, partner):
    rows = update.shape[0]
    n_around = lax.axis_size("az")
    radial_pos = lax.axis_index("sr")
    is_first = (radial_pos == 0).astype(jnp.float32)
    across = from_behind(update[0], "az", n_around // 2)
    lines = across.shape[0]
    picker = (partner[:, None] == lax.broadcasted_iota(jnp.int32, (lines, lines), 1)).astype(
        jnp.float32
    )
    polar = (
        jnp.einsum("kj,jvw->kvw", picker, across, precision=HIGH)
        * axis_flag.astype(jnp.float32)[:, None, None]
    )
    middle = with_halo(update, (("sr", 0),), 1, False)
    beside_all = with_halo(update, (("az", 1),), 1, True)
    first_row = middle[0] + is_first * polar
    last_row = middle[rows + 1]
    left = beside_all[:, :-2]
    right = beside_all[:, 2:]
    below = jnp.concatenate([first_row[None], middle[1:rows]], axis=0)
    above = jnp.concatenate([middle[2 : rows + 1], last_row[None]], axis=0)
    total = jnp.zeros_like(update)
    for direction, neighbour in enumerate((below, above, left, right)):
        total = total + jnp.einsum("ikab,ikbw->ikaw", off_jac[direction], neighbour, precision=HIGH)
    return total


def body(residual, dinv, wall_jac, lower_coef, upper_coef, off_jac, lengths, axis_flag, partner):
    points = residual.shape[-1]
    active = (
        lax.broadcasted_iota(jnp.int32, lengths.shape + (points,), 2) < lengths[:, :, None]
    ).astype(jnp.float32)
    update = jnp.zeros_like(residual)
    for sweep in range(SWEEPS):
        if sweep == 0:
            rhs = residual
        else:
            rhs = residual - neighbour_sum(update, off_jac, axis_flag, partner)
        update = solve_lines(rhs, dinv, wall_jac, lower_coef, upper_coef, active)
    next_rhs = residual - neighbour_sum(update, off_jac, axis_flag, partner)
    return (update, next_rhs)


def solution(mesh):
    in_specs = (
        P("sr", "az", None, None),
        P("sr", "az", None, None, None),
        P("sr", "az", None, None),
        P("sr", "az", None),
        P("sr", "az", None),
        P(None, "sr", "az", None, None),
        P("sr", "az"),
        P("az"),
        P("az"),
    )
    out_specs = (P("sr", "az", None, None), P("sr", "az", None, None))
    return jax.shard_map(body, mesh=mesh, in_specs=in_specs, out_specs=out_specs, check_vma=False)
```

profile of v0, /device:TPU:0, one launch (start us, length us, event | category | flops | bytes accessed | tf_op | source)
XLA Modules:
  0.0 87.3 jit_solution(16465485204678444752)
XLA Ops:
  0.6 2.0 %copy.38 = f32[4,16,10,10]{2,3,1,0:T(8,128)} copy(f32[4,16,10,10]{1,0,3,2:T(4,128)} %param.11) | data formatting | bytes 51200 | tf_op args[2]
  2.7 2.0 %copy.40 = f32[4,16,10,10]{3,2,1,0:T(8,128)} copy(f32[4,16,10,10]{1,0,3,2:T(4,128)} %param.11) | data formatting | bytes 51200 | tf_op args[2]
  4.7 0.8 fusion.78
  5.5 2.4 %multiply_reduce_fusion.9 = f32[4,16,128,10]{2,1,3,0:T(8,128)S(1)} fusion(f32[4,16,10,10,128]{4,1,3,2,0:T(8,128)} %param.10, f32[4,16,128,10]{2,1,3,0:T(8,128)} %bitcast.172), kind=kLoop, calls=%fused_computation.9 | loop fusion | flops 1556480 | bytes 3932160 | tf_op jit(solution)/shard_map/...abw,...bw->...aw/dot_general | solution.py:36
  8.4 1.3 %convolution_multiply_fusion.15 = f32[4,16,128,10]{2,3,1,0:T(8,128)S(1)} fusion(f32[4,16,10,10]{2,3,1,0:T(8,128)S(1)} %copy-done.1, f32[4,16,10,127]{3,2,1,0:T(8,128)S(1)} %copy.132, f32[4,16,128]{2,1,0:T(8,128)S(1)} %copy-done.13), kind=kOutput, calls=%fused_computation.67 | convolution fusion | flops 9912320 | bytes 711168 | tf_op jit(solution)/shard_map/...ab,...bw->...aw/dot_general | solution.py:44
  9.7 1.1 %fusion.37 = f32[4,16,128,10]{2,3,1,0:T(8,128)S(1)} fusion(f32[4,16,128,10]{2,3,1,0:T(8,128)S(1)} %convolution_multiply_fusion.15, f32[4,16,10,10]{3,2,1,0:T(8,128)S(1)} %copy-done.3, f32[4,16,10,128]{3,1,2,0:T(8,128)S(1)} %copy-done.5, f32[4,16,10,127]{3,2,1,0:T(8,128)S(1)} %copy.133, f32[4,16,128]{2,1,0:T(8,128)S(1)} %copy-done.14), kind=kOutput, calls=%fused_computation.66 | convolution fusion | flops 10076160 | bytes 1366528 | tf_op jit(solution)/shard_map/...ba,...bw->...aw/dot_general | solution.py:47
  11.6 1.3 %convolution_multiply_fusion.13 = f32[4,16,128,10]{2,3,1,0:T(8,128)S(1)} fusion(f32[4,16,10,10]{2,3,1,0:T(8,128)S(1)} %copy-done.1, f32[4,16,10,127]{3,2,1,0:T(8,128)S(1)} %copy.134, f32[4,16,128]{2,1,0:T(8,128)S(1)} %copy-done.13), kind=kOutput, calls=%fused_computation.61 | convolution fusion | flops 9912320 | bytes 711168 | tf_op jit(solution)/shard_map/...ab,...bw->...aw/dot_general | solution.py:44
  13.0 1.1 %fusion.33 = f32[4,16,128,10]{2,3,1,0:T(8,128)S(1)} fusion(f32[4,16,128,10]{2,3,1,0:T(8,128)S(1)} %convolution_multiply_fusion.13, f32[4,16,10,10]{3,2,1,0:T(8,128)S(1)} %copy-done.3, f32[4,16,10,128]{3,1,2,0:T(8,128)S(1)} %copy-done.5, f32[4,16,10,127]{3,2,1,0:T(8,128)S(1)} %copy.135, f32[4,16,128]{2,1,0:T(8,128)S(1)} %copy-done.14), kind=kOutput, calls=%fused_computation.60 | convolution fusion | flops 10076160 | bytes 1366528 | tf_op jit(solution)/shard_map/...ba,...bw->...aw/dot_general | solution.py:47
  14.9 1.3 %convolution_multiply_fusion.11 = f32[4,16,128,10]{2,3,1,0:T(8,128)S(1)} fusion(f32[4,16,10,10]{2,3,1,0:T(8,128)S(1)} %copy-done.1, f32[4,16,10,127]{3,2,1,0:T(8,128)S(1)} %copy.136, f32[4,16,128]{2,1,0:T(8,128)S(1)} %copy-done.13), kind=kOutput, calls=%fused_computation.55 | convolution fusion | flops 9912320 | bytes 711168 | tf_op jit(solution)/shard_map/...ab,...bw->...aw/dot_general | solution.py:44
  16.3 1.1 %fusion.29 = f32[4,16,128,10]{2,3,1,0:T(8,128)S(1)} fusion(f32[4,16,128,10]{2,3,1,0:T(8,128)S(1)} %convolution_multiply_fusion.11, f32[4,16,10,10]{3,2,1,0:T(8,128)S(1)} %copy-done.3, f32[4,16,10,128]{3,1,2,0:T(8,128)S(1)} %copy-done.5, f32[4,16,10,127]{3,2,1,0:T(8,128)S(1)} %copy.137, f32[4,16,128]{2,1,0:T(8,128)S(1)} %copy-done.14), kind=kOutput, calls=%fused_computation.54 | convolution fusion | flops 10076160 | bytes 1366528 | tf_op jit(solution)/shard_map/...ba,...bw->...aw/dot_general | solution.py:47
  18.2 1.3 %convolution_multiply_fusion.9 = f32[4,16,128,10]{2,3,1,0:T(8,128)S(1)} fusion(f32[4,16,10,10]{2,3,1,0:T(8,128)S(1)} %copy-done.1, f32[4,16,10,127]{3,2,1,0:T(8,128)S(1)} %copy.138, f32[4,16,128]{2,1,0:T(8,128)S(1)} %copy-done.13), kind=kOutput, calls=%fused_computation.49 | convolution fusion | flops 9912320 | bytes 711168 | tf_op jit(solution)/shard_map/...ab,...bw->...aw/dot_general | solution.py:44
  19.6 1.2 %fusion.25 = f32[4,16,128,10]{2,3,1,0:T(8,128)S(1)} fusion(f32[4,16,128,10]{2,3,1,0:T(8,128)S(1)} %convolution_multiply_fusion.9, f32[4,16,10,10]{3,2,1,0:T(8,128)S(1)} %copy-done.3, f32[4,16,10,128]{3,1,2,0:T(8,128)S(1)} %copy-done.5, f32[4,16,10,127]{3,2,1,0:T(8,128)S(1)} %copy.139, f32[4,16,128]{2,1,0:T(8,128)S(1)} %copy-done.14), kind=kOutput, calls=%fused_computation.48 | convolution fusion | flops 10076160 | bytes 1366528 | tf_op jit(solution)/shard_map/...ba,...bw->...aw/dot_general | solution.py:47
  21.4 0.8 fusion.110
  22.1 1.3 %collective-permute-start.2 = (f32[1,16,10,128]{3,1,2,0:T(8,128)S(1)}, f32[1,16,10,128]{3,1,2,0:T(8,128)S(1)}, u32[]{:S(2)}, u32[]{:S(2)}) collective-permute-start(f32[1,16,10,128]{3,1,2,0:T(8,128)S(1)} %get-tuple-element.31), channel_id=1, source_target_pairs={{8,0},{16,8},{24,16},{9,1},{17,9},{25,17},{10,2},{18,10},{26,18},{... | collective-permute-start | bytes 245768 | tf_op jit(solution)/shard_map/ppermute | solution.py:28
  23.4 6.1 %collective-permute-start = (f32[1,16,10,128]{3,1,2,0:T(8,128)}, f32[1,16,10,128]{3,1,2,0:T(8,128)}, u32[]{:S(2)}, u32[]{:S(2)}) collective-permute-start(f32[1,16,10,128]{3,1,2,0:T(8,128)} %get-tuple-element.33), channel_id=1, source_target_pairs={{0,8},{8,16},{16,24},{1,9},{9,17},{17,25},{2,10},{10,18},{18,26},{... | collective-permute-start | bytes 245768 | tf_op jit(solution)/shard_map/ppermute | solution.py:25
  29.5 3.1 %collective-permute-start.1 = (f32[16,10,128]{2,0,1:T(8,128)}, f32[16,10,128]{2,0,1:T(8,128)}, u32[]{:S(2)}, u32[]{:S(2)}) collective-permute-start(f32[16,10,128]{2,0,1:T(8,128)} %get-tuple-element.32), channel_id=1, source_target_pairs={{0,4},{1,5},{2,6},{3,7},{4,0},{5,1},{6,2},{7,3},{8,12},{9,13},{10,... | collective-permute-start | bytes 245768 | tf_op jit(solution)/shard_map/ppermute | solution.py:15
  33.3 3.5 %collective-permute-start.4 = (f32[4,1,10,128]{3,1,2,0:T(1,128)}, f32[4,1,10,128]{3,1,2,0:T(1,128)}, u32[]{:S(2)}, u32[]{:S(2)}) collective-permute-start(f32[4,1,10,128]{3,1,2,0:T(1,128)} %get-tuple-element.28), channel_id=1, source_target_pairs={{1,0},{2,1},{3,2},{4,3},{5,4},{6,5},{7,6},{0,7},{9,8},{10,9},{11,1... | collective-permute-start | bytes 61448 | tf_op jit(solution)/shard_map/ppermute | solution.py:28
  36.8 0.9 %fusion.100 = (f32[1,4,16,10,10]{2,1,4,3,0:T(4,128)}, f32[1,4,16,10,10]{2,1,4,3,0:T(4,128)}, f32[1,4,16,10,10]{2,1,4,3,0:T(4,128)}, f32[1,4,16,10,10]{2,1,4,3,0:T(4,128)}) fusion(f32[4,4,16,10,10]{2,1,4,3,0:T(4,128)S(1)} %copy-done.16), kind=kLoop, calls=%fused_computation.154 | loop fusion | bytes 204800 | tf_op jit(solution)/shard_map/slice | solution.py:78
  37.8 0.8 fusion.109
  38.6 2.1 %copy.118 = f32[1,4,16,10,10]{4,3,2,1,0:T(8,128)} copy(f32[1,4,16,10,10]{2,1,4,3,0:T(4,128)} %get-tuple-element.6) | data formatting | bytes 51200
  40.7 2.1 %copy.119 = f32[1,4,16,10,10]{4,3,2,1,0:T(8,128)} copy(f32[1,4,16,10,10]{2,1,4,3,0:T(4,128)} %get-tuple-element.5) | data formatting | bytes 51200
  42.8 2.1 %copy.121 = f32[1,4,16,10,10]{4,3,2,1,0:T(8,128)} copy(f32[1,4,16,10,10]{2,1,4,3,0:T(4,128)} %get-tuple-element.7) | data formatting | bytes 51200
  44.8 2.1 %copy.120 = f32[1,4,16,10,10]{4,3,2,1,0:T(8,128)} copy(f32[1,4,16,10,10]{2,1,4,3,0:T(4,128)} %get-tuple-element.4) | data formatting | bytes 51200
  46.9 1.3 %pad_maximum_fusion.3 = (f32[4,16,10,128]{3,1,2,0:T(8,128)S(1)}, f32[4,16,10,128]{3,1,2,0:T(8,128)S(1)}) fusion(f32[4,16,10,128]{3,1,2,0:T(8,128)} %copy-done.8, f32[4,1,10,128]{3,1,2,0:T(1,128)} %collective-permute-done.3, f32[4,1,10,128]{3,1,2,0:T(1,128)} %collective-permute-done.4), kind=kLoop, calls=%fused_computation.111 | loop fusion | flops 163840 | bytes 1024000 | tf_op jit(solution)/shard_map/concatenate | solution.py:29
  48.2 1.9 %fusion.58 = f32[4,16,128,10]{2,3,1,0:T(8,128)S(1)} fusion(f32[1,4,16,10,10]{4,3,2,1,0:T(8,128)} %copy.121, f32[4,16,10,128]{3,1,2,0:T(8,128)S(1)} %get-tuple-element.26), kind=kOutput, calls=%fused_computation.90 | convolution fusion | flops 9830400 | bytes 680960 | tf_op jit(solution)/shard_map/ikab,ikbw->ikaw/dot_general | solution.py:78
  50.1 1.2 %fusion.77 = f32[1,16,10,128]{3,1,2,0:T(8,128)S(1)} fusion(f32[1,16,10,128]{3,1,2,0:T(8,128)} %collective-permute-done, f32[16]{0:T(128)S(1)} %convert_element_type.19, f32[16,10,128]{2,0,1:T(8,128)} %collective-permute-done.1, f32[]{:T(128)S(6)} %convert_element_type.18, s32[16]{0:T(128)S(1)} %copy-done.17), kind=kOutput, calls=%fused_computation.129 | convolution fusion | flops 3993856 | bytes 245892 | tf_op jit(solution)/shard_map/kj,jvw->kvw/dot_general | solution.py:65
  51.3 1.0 %pad_maximum_fusion.4 = f32[4,16,10,128]{3,1,2,0:T(8,128)S(1)} fusion(f32[3,16,10,128]{3,1,2,0:T(8,128)} %get-tuple-element.30, f32[1,16,10,128]{3,1,2,0:T(8,128)S(1)} %fusion.77), kind=kLoop, calls=%fused_computation.112 | loop fusion | flops 81920 | bytes 655360 | tf_op jit(solution)/shard_map/concatenate | solution.py:74
  52.2 0.7 fusion.66
  53.1 0.7 convolution_add_fusion.3
  53.8 0.8 fusion.21
  55.8 1.3 %convolution_multiply_fusion.7 = f32[4,16,128,10]{2,3,1,0:T(8,128)S(1)} fusion(f32[4,16,10,10]{2,3,1,0:T(8,128)S(1)} %copy-done.2, f32[4,16,10,127]{3,2,1,0:T(8,128)S(1)} %copy.140, f32[4,16,128]{2,1,0:T(8,128)S(1)} %copy-done.13), kind=kOutput, calls=%fused_computation.38 | convolution fusion | flops 9912320 | bytes 711168 | tf_op jit(solution)/shard_map/...ab,...bw->...aw/dot_general | solution.py:44
  57.2 1.1 %fusion.18 = f32[4,16,128,10]{2,3,1,0:T(8,128)S(1)} fusion(f32[4,16,10,128]{3,2,1,0:T(8,128)S(1)} %fusion.21, f32[4,16,128,10]{2,3,1,0:T(8,128)S(1)} %convolution_multiply_fusion.7, f32[4,16,10,10]{3,2,1,0:T(8,128)S(1)} %copy-done.4, f32[4,16,10,127]{3,2,1,0:T(8,128)S(1)} %copy.141, f32[4,16,128]{2,1,0:T(8,128)S(1)} %copy-done.14), kind=kOutput, calls=%fused_computation.37 | convolution fusion | flops 10076160 | bytes 1366528 | tf_op jit(solution)/shard_map/...ba,...bw->...aw/dot_general | solution.py:47
  59.1 1.3 %convolution_multiply_fusion.5 = f32[4,16,128,10]{2,3,1,0:T(8,128)S(1)} fusion(f32[4,16,10,10]{2,3,1,0:T(8,128)S(1)} %copy-done.2, f32[4,16,10,127]{3,2,1,0:T(8,128)S(1)} %copy.142, f32[4,16,128]{2,1,0:T(8,128)S(1)} %copy-done.13), kind=kOutput, calls=%fused_computation.32 | convolution fusion | flops 9912320 | bytes 711168 | tf_op jit(solution)/shard_map/...ab,...bw->...aw/dot_general | solution.py:44
  60.5 1.1 %fusion.14 = f32[4,16,128,10]{2,3,1,0:T(8,128)S(1)} fusion(f32[4,16,10,128]{3,2,1,0:T(8,128)S(1)} %fusion.21, f32[4,16,128,10]{2,3,1,0:T(8,128)S(1)} %convolution_multiply_fusion.5, f32[4,16,10,10]{3,2,1,0:T(8,128)S(1)} %copy-done.4, f32[4,16,10,127]{3,2,1,0:T(8,128)S(1)} %copy.143, f32[4,16,128]{2,1,0:T(8,128)S(1)} %copy-done.14), kind=kOutput, calls=%fused_computation.31 | convolution fusion | flops 10076160 | bytes 1366528 | tf_op jit(solution)/shard_map/...ba,...bw->...aw/dot_general | solution.py:47
  62.4 1.5 %convolution_multiply_fusion.3 = f32[4,16,128,10]{2,3,1,0:T(8,128)S(1)} fusion(f32[4,16,10,10]{2,3,1,0:T(8,128)S(1)} %copy-done.2, f32[4,16,10,127]{3,2,1,0:T(8,128)S(1)} %copy.144, f32[4,16,128]{2,1,0:T(8,128)S(1)} %copy-done.13), kind=kOutput, calls=%fused_computation.26 | convolution fusion | flops 9912320 | bytes 711168 | tf_op jit(solution)/shard_map/...ab,...bw->...aw/dot_general | solution.py:44
  64.0 1.1 %fusion.10 = f32[4,16,128,10]{2,3,1,0:T(8,128)S(1)} fusion(f32[4,16,10,128]{3,2,1,0:T(8,128)S(1)} %fusion.21, f32[4,16,128,10]{2,3,1,0:T(8,128)S(1)} %convolution_multiply_fusion.3, f32[4,16,10,10]{3,2,1,0:T(8,128)S(1)} %copy-done.4, f32[4,16,10,127]{3,2,1,0:T(8,128)S(1)} %copy.145, f32[4,16,128]{2,1,0:T(8,128)S(1)} %copy-done.14), kind=kOutput, calls=%fused_computation.25 | convolution fusion | flops 10076160 | bytes 1366528 | tf_op jit(solution)/shard_map/...ba,...bw->...aw/dot_general | solution.py:47
  65.9 1.3 %convolution_multiply_fusion.1 = f32[4,16,128,10]{2,3,1,0:T(8,128)S(1)} fusion(f32[4,16,10,10]{2,3,1,0:T(8,128)S(1)} %copy-done.2, f32[4,16,10,127]{3,2,1,0:T(8,128)S(1)} %copy.146, f32[4,16,128]{2,1,0:T(8,128)S(1)} %copy-done.13), kind=kOutput, calls=%fused_computation.20 | convolution fusion | flops 9912320 | bytes 711168 | tf_op jit(solution)/shard_map/...ab,...bw->...aw/dot_general | solution.py:44
  67.3 1.1 %fusion.6 = f32[4,16,128,10]{2,3,1,0:T(8,128)S(1)} fusion(f32[4,16,10,128]{3,2,1,0:T(8,128)S(1)} %fusion.21, f32[4,16,128,10]{2,3,1,0:T(8,128)S(1)} %convolution_multiply_fusion.1, f32[4,16,10,10]{3,2,1,0:T(8,128)S(1)} %copy-done.4, f32[4,16,10,127]{3,2,1,0:T(8,128)S(1)} %copy.147, f32[4,16,128]{2,1,0:T(8,128)S(1)} %copy-done.14), kind=kOutput, calls=%fused_computation.19 | convolution fusion | flops 10076160 | bytes 1366528 | tf_op jit(solution)/shard_map/...ba,...bw->...aw/dot_general | solution.py:47
  69.1 3.5 %collective-permute-start.9 = (f32[4,1,10,128]{3,1,2,0:T(1,128)S(1)}, f32[4,1,10,128]{3,1,2,0:T(1,128)S(1)}, u32[]{:S(2)}, u32[]{:S(2)}) collective-permute-start(f32[4,1,10,128]{3,1,2,0:T(1,128)S(1)} %get-tuple-element.11), channel_id=1, source_target_pairs={{1,0},{2,1},{3,2},{4,3},{5,4},{6,5},{7,6},{0,7},{9,8},{10,9},{11,1... | collective-permute-start | bytes 61448 | tf_op jit(solution)/shard_map/ppermute | solution.py:28
  72.6 1.3 %collective-permute-start.7 = (f32[1,16,10,128]{3,1,2,0:T(8,128)S(1)}, f32[1,16,10,128]{3,1,2,0:T(8,128)S(1)}, u32[]{:S(2)}, u32[]{:S(2)}) collective-permute-start(f32[1,16,10,128]{3,1,2,0:T(8,128)S(1)} %get-tuple-element.14), channel_id=1, source_target_pairs={{8,0},{16,8},{24,16},{9,1},{17,9},{25,17},{10,2},{18,10},{26,18},{... | collective-permute-start | bytes 245768 | tf_op jit(solution)/shard_map/ppermute | solution.py:28
  73.9 4.6 %collective-permute-start.5 = (f32[1,16,10,128]{3,1,2,0:T(8,128)S(1)}, f32[1,16,10,128]{3,1,2,0:T(8,128)S(1)}, u32[]{:S(2)}, u32[]{:S(2)}) collective-permute-start(f32[1,16,10,128]{3,1,2,0:T(8,128)S(1)} %get-tuple-element.16), channel_id=1, source_target_pairs={{0,8},{8,16},{16,24},{1,9},{9,17},{17,25},{2,10},{10,18},{18,26},{... | collective-permute-start | bytes 245768 | tf_op jit(solution)/shard_map/ppermute | solution.py:25
  78.7 0.7 fusion.56
  79.4 1.1 %collective-permute-done.5 = f32[1,16,10,128]{3,1,2,0:T(8,128)S(1)} collective-permute-done((f32[1,16,10,128]{3,1,2,0:T(8,128)S(1)}, f32[1,16,10,128]{3,1,2,0:T(8,128)S(1)}, u32[]{:S(2)}, u32[]{:S(2)}) %collective-permute-start.5) | collective-permute-done | bytes 81952 | tf_op jit(solution)/shard_map/ppermute | solution.py:25
  80.5 3.4 %collective-permute-done.6 = f32[16,10,128]{2,0,1:T(8,128)S(1)} collective-permute-done((f32[16,10,128]{2,0,1:T(8,128)S(1)}, f32[16,10,128]{2,0,1:T(8,128)S(1)}, u32[]{:S(2)}, u32[]{:S(2)}) %collective-permute-start.6) | collective-permute-done | bytes 81952 | tf_op jit(solution)/shard_map/ppermute | solution.py:15
  84.2 0.7 fusion.64
  85.0 0.7 convolution_add_fusion.1
  85.7 0.8 fusion.2
  86.5 0.8 copy.29
  (111 shorter events, 9.5 us)
Async XLA Ops:
  5.5 2.9 %copy-start.1 = (f32[4,16,10,10]{2,3,1,0:T(8,128)S(1)}, f32[4,16,10,10]{2,3,1,0:T(8,128)}, u32[]{:S(2)}) copy-start(f32[4,16,10,10]{2,3,1,0:T(8,128)} %copy.38) | copy-start | bytes 76804
  5.5 2.9 %copy-start.13 = (f32[4,16,128]{2,1,0:T(8,128)S(1)}, f32[4,16,128]{2,1,0:T(8,128)}, u32[]{:S(2)}) copy-start(f32[4,16,128]{2,1,0:T(8,128)} %param.12) | copy-start | bytes 98308
  7.9 1.8 %copy-start.3 = (f32[4,16,10,10]{3,2,1,0:T(8,128)S(1)}, f32[4,16,10,10]{3,2,1,0:T(8,128)}, u32[]{:S(2)}) copy-start(f32[4,16,10,10]{3,2,1,0:T(8,128)} %copy.40) | copy-start | bytes 76804
  7.9 1.8 %copy-start.5 = (f32[4,16,10,128]{3,1,2,0:T(8,128)S(1)}, f32[4,16,10,128]{3,1,2,0:T(8,128)}, u32[]{:S(2)}) copy-start(f32[4,16,10,128]{3,1,2,0:T(8,128)} %param.9) | copy-start | bytes 983044
  7.9 1.8 %copy-start.14 = (f32[4,16,128]{2,1,0:T(8,128)S(1)}, f32[4,16,128]{2,1,0:T(8,128)}, u32[]{:S(2)}) copy-start(f32[4,16,128]{2,1,0:T(8,128)} %param.13) | copy-start | bytes 98308
  8.1 2.8 %copy-start = (f32[4,16,10,10,128]{4,1,3,2,0:T(8,128)S(1)}, f32[4,16,10,10,128]{4,1,3,2,0:T(8,128)}, u32[]{:S(2)}) copy-start(f32[4,16,10,10,128]{4,1,3,2,0:T(8,128)} %param.10) | copy-start | bytes 9830404
  20.8 16.0 %copy-start.16 = (f32[4,4,16,10,10]{2,1,4,3,0:T(4,128)S(1)}, f32[4,4,16,10,10]{2,1,4,3,0:T(4,128)}, u32[]{:S(2)}) copy-start(f32[4,4,16,10,10]{2,1,4,3,0:T(4,128)} %param.14) | copy-start | bytes 307204
  20.9 17.7 %copy-start.18 = (s32[16]{0:T(128)S(1)}, s32[16]{0:T(128)}, u32[]{:S(2)}) copy-start(s32[16]{0:T(128)} %param.16) | copy-start | bytes 196
  21.4 16.4 %copy-start.8 = (f32[4,16,10,128]{3,1,2,0:T(8,128)}, f32[4,16,10,128]{3,1,2,0:T(8,128)S(1)}, u32[]{:S(2)}) copy-start(f32[4,16,10,128]{3,1,2,0:T(8,128)S(1)} %multiply_bitcast_fusion.5) | copy-start | bytes 983044
  22.1 30.9 %collective-permute-start.2 = (f32[1,16,10,128]{3,1,2,0:T(8,128)S(1)}, f32[1,16,10,128]{3,1,2,0:T(8,128)S(1)}, u32[]{:S(2)}, u32[]{:S(2)}) collective-permute-start(f32[1,16,10,128]{3,1,2,0:T(8,128)S(1)} %get-tuple-element.31), channel_id=1, source_target_pairs={{8,0},{16,8},{24,16},{9,1},{17,9},{25,17},{10,2},{18,10},{26,18},{... | collective-permute-start | bytes 245768 | tf_op jit(solution)/shard_map/ppermute | solution.py:28
  23.4 26.6 %collective-permute-start = (f32[1,16,10,128]{3,1,2,0:T(8,128)}, f32[1,16,10,128]{3,1,2,0:T(8,128)}, u32[]{:S(2)}, u32[]{:S(2)}) collective-permute-start(f32[1,16,10,128]{3,1,2,0:T(8,128)} %get-tuple-element.33), channel_id=1, source_target_pairs={{0,8},{8,16},{16,24},{1,9},{9,17},{17,25},{2,10},{10,18},{18,26},{... | collective-permute-start | bytes 245768 | tf_op jit(solution)/shard_map/ppermute | solution.py:25
  29.5 20.5 %collective-permute-start.1 = (f32[16,10,128]{2,0,1:T(8,128)}, f32[16,10,128]{2,0,1:T(8,128)}, u32[]{:S(2)}, u32[]{:S(2)}) collective-permute-start(f32[16,10,128]{2,0,1:T(8,128)} %get-tuple-element.32), channel_id=1, source_target_pairs={{0,4},{1,5},{2,6},{3,7},{4,0},{5,1},{6,2},{7,3},{8,12},{9,13},{10,... | collective-permute-start | bytes 245768 | tf_op jit(solution)/shard_map/ppermute | solution.py:15
  33.3 13.6 %collective-permute-start.3 = (f32[4,1,10,128]{3,1,2,0:T(1,128)}, f32[4,1,10,128]{3,1,2,0:T(1,128)}, u32[]{:S(2)}, u32[]{:S(2)}) collective-permute-start(f32[4,1,10,128]{3,1,2,0:T(1,128)} %get-tuple-element.27), channel_id=1, source_target_pairs={{0,1},{1,2},{2,3},{3,4},{4,5},{5,6},{6,7},{7,0},{8,9},{9,10},{10,1... | collective-permute-start | bytes 61448 | tf_op jit(solution)/shard_map/ppermute | solution.py:25
  33.3 13.6 %collective-permute-start.4 = (f32[4,1,10,128]{3,1,2,0:T(1,128)}, f32[4,1,10,128]{3,1,2,0:T(1,128)}, u32[]{:S(2)}, u32[]{:S(2)}) collective-permute-start(f32[4,1,10,128]{3,1,2,0:T(1,128)} %get-tuple-element.28), channel_id=1, source_target_pairs={{1,0},{2,1},{3,2},{4,3},{5,4},{6,5},{7,6},{0,7},{9,8},{10,9},{11,1... | collective-permute-start | bytes 61448 | tf_op jit(solution)/shard_map/ppermute | solution.py:28
  37.8 12.3 %copy-start.17 = (s32[16]{0:T(128)S(1)}, s32[16]{0:T(128)}, u32[]{:S(2)}) copy-start(s32[16]{0:T(128)} %param.17) | copy-start | bytes 196
  46.9 5.4 %copy-start.9 = (f32[1,4,16,10,10]{4,3,2,1,0:T(8,128)S(1)}, f32[1,4,16,10,10]{4,3,2,1,0:T(8,128)}, u32[]{:S(2)}) copy-start(f32[1,4,16,10,10]{4,3,2,1,0:T(8,128)} %copy.118) | copy-start | bytes 76804
  46.9 6.1 %copy-start.15 = (f32[3,16,10,128]{3,1,2,0:T(8,128)S(1)}, f32[3,16,10,128]{3,1,2,0:T(8,128)}, u32[]{:S(2)}) copy-start(f32[3,16,10,128]{3,1,2,0:T(8,128)} %get-tuple-element.29) | copy-start | bytes 737284
  46.9 6.2 %copy-start.11 = (f32[1,4,16,10,10]{4,3,2,1,0:T(8,128)S(1)}, f32[1,4,16,10,10]{4,3,2,1,0:T(8,128)}, u32[]{:S(2)}) copy-start(f32[1,4,16,10,10]{4,3,2,1,0:T(8,128)} %copy.119) | copy-start | bytes 76804
  48.2 5.6 %copy-start.6 = (f32[4,16,10,128]{3,1,2,0:T(8,128)S(1)}, f32[4,16,10,128]{3,1,2,0:T(8,128)}, u32[]{:S(2)}) copy-start(f32[4,16,10,128]{3,1,2,0:T(8,128)} %param.9) | copy-start | bytes 983044
  48.2 5.6 %copy-start.12 = (f32[1,4,16,10,10]{4,3,2,1,0:T(8,128)S(1)}, f32[1,4,16,10,10]{4,3,2,1,0:T(8,128)}, u32[]{:S(2)}) copy-start(f32[1,4,16,10,10]{4,3,2,1,0:T(8,128)} %copy.120) | copy-start | bytes 76804
  54.8 1.0 %copy-start.2 = (f32[4,16,10,10]{2,3,1,0:T(8,128)S(1)}, f32[4,16,10,10]{2,3,1,0:T(8,128)}, u32[]{:S(2)}) copy-start(f32[4,16,10,10]{2,3,1,0:T(8,128)} %copy.38) | copy-start | bytes 76804
  55.2 2.0 %copy-start.4 = (f32[4,16,10,10]{3,2,1,0:T(8,128)S(1)}, f32[4,16,10,10]{3,2,1,0:T(8,128)}, u32[]{:S(2)}) copy-start(f32[4,16,10,10]{3,2,1,0:T(8,128)} %copy.40) | copy-start | bytes 76804
  68.5 10.2 %copy-start.10 = (f32[1,4,16,10,10]{4,3,2,1,0:T(8,128)S(1)}, f32[1,4,16,10,10]{4,3,2,1,0:T(8,128)}, u32[]{:S(2)}) copy-start(f32[1,4,16,10,10]{4,3,2,1,0:T(8,128)} %copy.121) | copy-start | bytes 76804
  68.9 16.0 %copy-start.7 = (f32[4,16,10,128]{3,1,2,0:T(8,128)}, f32[4,16,10,128]{3,1,2,0:T(8,128)S(1)}, u32[]{:S(2)}) copy-start(f32[4,16,10,128]{3,1,2,0:T(8,128)S(1)} %multiply_bitcast_fusion) | copy-start | bytes 983044
  69.0 9.6 %collective-permute-start.8 = (f32[4,1,10,128]{3,1,2,0:T(1,128)S(1)}, f32[4,1,10,128]{3,1,2,0:T(1,128)S(1)}, u32[]{:S(2)}, u32[]{:S(2)}) collective-permute-start(f32[4,1,10,128]{3,1,2,0:T(1,128)S(1)} %get-tuple-element.10), channel_id=1, source_target_pairs={{0,1},{1,2},{2,3},{3,4},{4,5},{5,6},{6,7},{7,0},{8,9},{9,10},{10,1... | collective-permute-start | bytes 61448 | tf_op jit(solution)/shard_map/ppermute | solution.py:25
  69.1 9.5 %collective-permute-start.9 = (f32[4,1,10,128]{3,1,2,0:T(1,128)S(1)}, f32[4,1,10,128]{3,1,2,0:T(1,128)S(1)}, u32[]{:S(2)}, u32[]{:S(2)}) collective-permute-start(f32[4,1,10,128]{3,1,2,0:T(1,128)S(1)} %get-tuple-element.11), channel_id=1, source_target_pairs={{1,0},{2,1},{3,2},{4,3},{5,4},{6,5},{7,6},{0,7},{9,8},{10,9},{11,1... | collective-permute-start | bytes 61448 | tf_op jit(solution)/shard_map/ppermute | solution.py:28
  72.6 12.3 %collective-permute-start.7 = (f32[1,16,10,128]{3,1,2,0:T(8,128)S(1)}, f32[1,16,10,128]{3,1,2,0:T(8,128)S(1)}, u32[]{:S(2)}, u32[]{:S(2)}) collective-permute-start(f32[1,16,10,128]{3,1,2,0:T(8,128)S(1)} %get-tuple-element.14), channel_id=1, source_target_pairs={{8,0},{16,8},{24,16},{9,1},{17,9},{25,17},{10,2},{18,10},{26,18},{... | collective-permute-start | bytes 245768 | tf_op jit(solution)/shard_map/ppermute | solution.py:28
  73.9 6.6 %collective-permute-start.5 = (f32[1,16,10,128]{3,1,2,0:T(8,128)S(1)}, f32[1,16,10,128]{3,1,2,0:T(8,128)S(1)}, u32[]{:S(2)}, u32[]{:S(2)}) collective-permute-start(f32[1,16,10,128]{3,1,2,0:T(8,128)S(1)} %get-tuple-element.16), channel_id=1, source_target_pairs={{0,8},{8,16},{16,24},{1,9},{9,17},{17,25},{2,10},{10,18},{18,26},{... | collective-permute-start | bytes 245768 | tf_op jit(solution)/shard_map/ppermute | solution.py:25
  78.5 5.4 %collective-permute-start.6 = (f32[16,10,128]{2,0,1:T(8,128)S(1)}, f32[16,10,128]{2,0,1:T(8,128)S(1)}, u32[]{:S(2)}, u32[]{:S(2)}) collective-permute-start(f32[16,10,128]{2,0,1:T(8,128)S(1)} %get-tuple-element.15), channel_id=1, source_target_pairs={{0,4},{1,5},{2,6},{3,7},{4,0},{5,1},{6,2},{7,3},{8,12},{9,13},{10,... | collective-permute-start | bytes 245768 | tf_op jit(solution)/shard_map/ppermute | solution.py:15
where the time goes:
time: 87.8 us; the launch traced here: 87.3 us
  matrix products  27.6 us (31%)
  starting transfers between devices  23.5 us (27%)
  local copies, waits for them, and re-layouts  20.9 us (24%)
  other arithmetic  9.33 us (11%)
  waiting for transfers between devices  4.47 us (5%)
  between operations  1.51 us (2%)
    unnamed x70, local copies, waits for them, and re-layouts  16.3 us
    ppermute x4, starting transfers between devices, with_halo(): lax.ppermute(lax.slice_in_dim(block, block.shape[dim] - width, None, axis...  10.7 us
    dot_general x8, matrix products, solve_lines(): jnp.einsum('...ab,...bw->...aw', wall_jac, below, precision=HIGH)  10.3 us
    ppermute x4, starting transfers between devices, with_halo(): lax.ppermute(lax.slice_in_dim(block, 0, width, axis=dim), axis, backward)  9.64 us
    dot_general x8, matrix products, solve_lines(): jnp.einsum('...ba,...bw->...aw', wall_jac, above, precision=HIGH)  8.69 us
    dot_general x8, matrix products, neighbour_sum(): jnp.einsum('ikab,ikbw->ikaw', off_jac[direction], neighbour, precision=HIGH)  7.19 us
    dot_general x10, other arithmetic, apply_inverse(): return jnp.einsum('...abw,...bw->...aw', dinv, vec, precision=HIGH)  5.9 us
    ppermute x2, waiting for transfers between devices, from_behind(): lax.ppermute(value, axis, [(i, (i + by) % size) for i in range(size)])  3.37 us
  transfers between devices with their start and end apart: 10, of which 2 were waited for; matrix products, arithmetic and copies ran while one was open for 21% of the time, Pallas kernels for 0%

commit v1 on v0

v1 whole, which is shorter than its diff:
```python
import functools
import jax
import jax.numpy as jnp
from jax import lax
from jax.experimental import pallas as pl
from jax.experimental.pallas import tpu as pltpu
from jax.sharding import PartitionSpec as P

INNER = 4
SUB = 8
MESH = pl.DeviceIdType.MESH


def transpose_in(ref, lead, out_store, nv):
    block = ref[lead + (slice(0, SUB),)]
    turned = jnp.swapaxes(block, 0, 1)
    for b in range(SUB):
        out_store(b, turned[b])
    for b in range(SUB, nv):
        out_store(b, ref[lead + (b,)])


def kernel(sizes, res_hbm, dinv_hbm, wall_ref, low_ref, up_ref, off_ref, len_ref, pick_ref,
           upd_ref, next_ref,
           dnat, dtab, jtab, otab, rtab, rhs, lowm, upm, act, u, polar, left_out, right_out,
           left_in, right_in, rnat, load_sem, send_sem, recv_sem):
    n_sr, n_az, rows, lines, nv, points = sizes
    halves = lines // SUB
    groups = rows * halves
    sr, az = lax.axis_index("sr"), lax.axis_index("az")
    west, east = lax.rem(az + n_az - 1, n_az), lax.rem(az + 1, n_az)
    across = lax.rem(az + n_az // 2, n_az)
    last = n_sr - 1

    barrier = pltpu.get_barrier_semaphore()

    def greet(dst):
        pl.semaphore_signal(barrier, inc=1, device_id=dst, device_id_type=MESH)

    greet((sr, west))
    greet((sr, east))

    @pl.when(sr > 0)
    def _():
        greet((sr - 1, az))

    @pl.when(sr < last)
    def _():
        greet((sr + 1, az))

    @pl.when(sr == 0)
    def _():
        greet((0, across))

    def load(i):
        return pltpu.make_async_copy(dinv_hbm.at[i], dnat.at[i], load_sem.at[i])

    res_copy = pltpu.make_async_copy(res_hbm, rnat, load_sem.at[rows])
    res_copy.start()
    for i in range(rows):
        load(i).start()

    lane = lax.broadcasted_iota(jnp.int32, (SUB, points), 1)

    def place(g):
        return lax.div(g, halves), pl.multiple_of(lax.rem(g, halves) * SUB, SUB)

    @pl.when(sr == last)
    def _():
        u[0, rows + 1] = jnp.zeros(u.shape[2:], jnp.float32)
        u[1, rows + 1] = jnp.zeros(u.shape[2:], jnp.float32)

    @pl.loop(0, groups)
    def _(g):
        i, k = place(g)
        eight = pl.ds(k, SUB)
        lowm[g] = jnp.where(lane > 0, low_ref[i, eight, :], 0.0)
        upm[g] = jnp.where(lane < points - 1, up_ref[i, eight, :], 0.0)
        act[g] = (lane < len_ref[i, eight, :]).astype(jnp.float32)
        for a in range(nv):
            row = wall_ref[i, eight, a, :]
            for b in range(nv):
                jtab[g, a * nv + b] = jnp.broadcast_to(row[:, b:b + 1], (SUB, points))
        for d in range(4):
            for a in range(nv):
                otab[g, d * nv + a, :, 0:nv] = off_ref[d, i, eight, a, :]

    res_copy.wait()

    @pl.loop(0, groups)
    def _(g):
        i, k = place(g)
        for a in range(nv):
            rtab[g, a] = rnat[i, pl.ds(k, SUB), a, :]

    for i in range(rows):
        load(i).wait()

    @pl.loop(0, groups)
    def _(g):
        i, k = place(g)
        for a in range(nv):
            def put(b, value, a=a):
                dtab[g, a * nv + b] = value
            block = jnp.swapaxes(dnat[i, pl.ds(k, SUB), a, 0:SUB, :], 0, 1)
            for b in range(SUB):
                put(b, block[b])
            for b in range(SUB, nv):
                put(b, dnat[i, pl.ds(k, SUB), a, b, :])

    def inverse(g, vec):
        out = []
        for a in range(nv):
            total = dtab[g, a * nv] * vec[0]
            for b in range(1, nv):
                total = total + dtab[g, a * nv + b] * vec[b]
            out.append(total * act[g])
        return out

    def solve(slot, right_side):
        @pl.loop(0, groups)
        def _(g):
            i, k = place(g)

            def step(_, x):
                below = [lowm[g] * pltpu.roll(v, 1, 1) for v in x]
                above = [upm[g] * pltpu.roll(v, points - 1, 1) for v in x]
                cross = [right_side[g, a] for a in range(nv)]
                for b in range(nv):
                    for a in range(nv):
                        cross[a] = cross[a] - jtab[g, a * nv + b] * below[b]
                        cross[a] = cross[a] - jtab[g, b * nv + a] * above[b]
                return tuple(inverse(g, cross))

            x = tuple(inverse(g, [right_side[g, a] for a in range(nv)]))
            x = lax.fori_loop(0, INNER, step, x)
            for a in range(nv):
                u[slot, i + 1, a, pl.ds(pl.multiple_of(k + SUB, SUB), SUB), :] = x[a]

    def exchange(slot):
        for i in range(rows):
            for a in range(nv):
                left_out[slot, i, a] = u[slot, i + 1, a, SUB]
                right_out[slot, i, a] = u[slot, i + 1, a, SUB + lines - 1]

        def copy(src, dst, kind, dev):
            return pltpu.make_async_remote_copy(
                src_ref=src, dst_ref=dst, send_sem=send_sem.at[slot, kind],
                recv_sem=recv_sem.at[slot, kind], device_id=dev, device_id_type=MESH)

        mid = pl.ds(SUB, lines)
        first, final = u.at[slot, 1, :, mid], u.at[slot, rows, :, mid]
        to_west = copy(left_out.at[slot], right_in.at[slot], 0, (sr, west))
        to_east = copy(right_out.at[slot], left_in.at[slot], 1, (sr, east))
        down = copy(first, u.at[slot, rows + 1, :, mid], 2, (jnp.maximum(sr - 1, 0), az))
        upward = copy(final, u.at[slot, 0, :, mid], 3, (jnp.minimum(sr + 1, last), az))
        over = copy(first, polar.at[slot], 4, (0, across))

        @pl.when(sr == 0)
        def _():
            over.start()

        @pl.when(sr > 0)
        def _():
            down.start()

        @pl.when(sr < last)
        def _():
            upward.start()

        to_west.start()
        to_east.start()

        to_west.wait()
        to_east.wait()
        for i in range(rows):
            for a in range(nv):
                u[slot, i + 1, a, SUB - 1] = left_in[slot, i, a]
                u[slot, i + 1, a, SUB + lines] = right_in[slot, i, a]

        @pl.when(sr > 0)
        def _():
            down.wait_send()
            upward.wait_recv()

        @pl.when(sr < last)
        def _():
            upward.wait_send()
            down.wait_recv()

        @pl.when(sr == 0)
        def _():
            over.wait()
            for a in range(nv):
                u[slot, 0, a, mid] = jnp.dot(
                    pick_ref[...], polar[slot, a], precision=lax.Precision.HIGHEST,
                    preferred_element_type=jnp.float32)

    def residual_less(slot, store):
        @pl.loop(0, rows)
        def _(i):
            for half in range(halves):
                g = i * halves + half
                base = SUB + half * SUB
                acc = [rtab[g, a] for a in range(nv)]
                for d, (di, dk) in enumerate(((0, 0), (2, 0), (1, -1), (1, 1))):
                    near = [u[slot, i + di, b, base + dk:base + dk + SUB] for b in range(nv)]
                    for a in range(nv):
                        coef = otab[g, d * nv + a]
                        for b in range(nv):
                            acc[a] = acc[a] - jnp.broadcast_to(
                                coef[:, b:b + 1], (SUB, points)) * near[b]
                store(g, i, half, acc)

    def keep(g, i, half, acc):
        for a in range(nv):
            rhs[g, a] = acc[a]

    def finish(g, i, half, acc):
        for a in range(nv):
            next_ref[a, i, half * SUB:(half + 1) * SUB, :] = acc[a]

    solve(0, rtab)

    @pl.when(sr == last)
    def _():
        pl.semaphore_wait(barrier, 3)

    @pl.when(sr < last)
    def _():
        pl.semaphore_wait(barrier, 4)

    exchange(0)
    residual_less(0, keep)
    solve(1, rhs)
    exchange(1)
    for i in range(rows):
        for a in range(nv):
            upd_ref[a, i] = u[1, i + 1, a, SUB:SUB + lines, :]
    residual_less(1, finish)


def body(mesh_sizes, residual, dinv, wall_jac, lower_coef, upper_coef, off_jac, lengths, axis_flag, partner):
    rows, lines, nv, points = residual.shape
    n_sr, n_az = mesh_sizes
    groups = rows * (lines // SUB)
    sizes = (n_sr, n_az, rows, lines, nv, points)
    pick = jnp.where(
        partner[:, None] == lax.broadcasted_iota(jnp.int32, (lines, lines), 1),
        axis_flag[:, None].astype(jnp.float32), 0.0)
    vmem = pl.BlockSpec(memory_space=pltpu.VMEM)
    hbm = pl.BlockSpec(memory_space=pl.ANY)
    out = jax.ShapeDtypeStruct((nv, rows, lines, points), jnp.float32)
    f32 = jnp.float32
    update, next_rhs = pl.pallas_call(
        functools.partial(kernel, sizes),
        out_shape=(out, out),
        in_specs=[hbm, hbm, vmem, vmem, vmem, vmem, vmem, vmem],
        out_specs=(vmem, vmem),
        scratch_shapes=[
            pltpu.VMEM((rows, lines, nv, nv, points), f32),
            pltpu.VMEM((groups, nv * nv, SUB, points), f32),
            pltpu.VMEM((groups, nv * nv, SUB, points), f32),
            pltpu.VMEM((groups, 4 * nv, SUB, 128), f32),
            pltpu.VMEM((groups, nv, SUB, points), f32),
            pltpu.VMEM((groups, nv, SUB, points), f32),
            pltpu.VMEM((groups, SUB, points), f32),
            pltpu.VMEM((groups, SUB, points), f32),
            pltpu.VMEM((groups, SUB, points), f32),
            pltpu.VMEM((2, rows + 2, nv, lines + 2 * SUB, points), f32),
            pltpu.VMEM((2, nv, lines, points), f32),
            pltpu.VMEM((2, rows, nv, points), f32),
            pltpu.VMEM((2, rows, nv, points), f32),
            pltpu.VMEM((2, rows, nv, points), f32),
            pltpu.VMEM((2, rows, nv, points), f32),
            pltpu.VMEM((rows, lines, nv, points), f32),
            pltpu.SemaphoreType.DMA((rows + 1,)),
            pltpu.SemaphoreType.DMA((2, 5)),
            pltpu.SemaphoreType.DMA((2, 5)),
        ],
        compiler_params=pltpu.CompilerParams(
            collective_id=0, has_side_effects=True, vmem_limit_bytes=48 * 2**20),
    )(residual, dinv, wall_jac, lower_coef, upper_coef, off_jac, lengths[:, :, None], pick)
    back = (1, 2, 0, 3)
    return update.transpose(back), next_rhs.transpose(back)


def solution(mesh):
    in_specs = (
        P("sr", "az", None, None),
        P("sr", "az", None, None, None),
        P("sr", "az", None, None),
        P("sr", "az", None),
        P("sr", "az", None),
        P(None, "sr", "az", None, None),
        P("sr", "az"),
        P("az"),
        P("az"),
    )
    out_specs = (P("sr", "az", None, None), P("sr", "az", None, None))
    sizes = (mesh.shape["sr"], mesh.shape["az"])
    return jax.shard_map(functools.partial(body, sizes), mesh=mesh, in_specs=in_specs,
                         out_specs=out_specs, check_vma=False)
```

time: 87.8 us -> 61.4 us (0.70)
  Pallas kernels: 0 us -> 46.9 us
  matrix products: 27.6 us -> 0 us
  starting transfers between devices: 23.5 us -> 0 us
  local copies, waits for them, and re-layouts: 20.9 us -> 12.2 us
  other arithmetic: 9.33 us -> 1.38 us
  waiting for transfers between devices: 4.47 us -> 0 us
    pallas_call x0 -> x1, Pallas kernels: none -> 46.9 us  [body(): pl.pallas_call(functools.partial(kernel, sizes), out_shape=(out, out), in...]
    dot_general x26 -> x0, matrix products: 27.6 us -> none  [the longest x8 10.3 us: solve_lines(): jnp.einsum('...ab,...bw->...aw', wall_jac, below, precision=HIGH)]
    ppermute x10 -> x0, starting transfers between devices: 23.5 us -> none  [the longest x4 10.7 us: with_halo(): lax.ppermute(lax.slice_in_dim(block, block.shape[dim] - width, None, axis...]
    dot_general x10 -> x0, other arithmetic: 5.9 us -> none  [apply_inverse(): return jnp.einsum('...abw,...bw->...aw', dinv, vec, precision=HIGH)]
    unnamed x70 -> x10, local copies, waits for them, and re-layouts: 16.3 us -> 11.4 us
    slice x15 -> x0, local copies, waits for them, and re-layouts: 4.53 us -> none  [the longest x8 1.28 us: solve_lines(): above = jnp.concatenate([update[..., 1:], zeros], axis=-1)]
    ppermute x10 -> x0, waiting for transfers between devices: 4.47 us -> none  [the longest x2 3.37 us: from_behind(): lax.ppermute(value, axis, [(i, (i + by) % size) for i in range(size)])]
    concatenate x6 -> x0, other arithmetic: 2.39 us -> none  [the longest x2 1.35 us: with_halo(): block = jnp.concatenate([low, block, high], axis=dim)]
  transfers between devices with their start and end apart: 10 -> 0, of which waited for: 2 -> 0; matrix products, arithmetic and copies ran while one was open for 21% -> 0% of each run, Pallas kernels for 0% -> 0%
where the time goes in v1:
time: 61.4 us; the launch traced here: 61.1 us
  Pallas kernels  46.9 us (76%)
  local copies, waits for them, and re-layouts  12.2 us (20%)
  other arithmetic  1.38 us (2%)
  between operations  0.67 us (1%)
    pallas_call x1, Pallas kernels, body(): pl.pallas_call(functools.partial(kernel, sizes), out_shape=(out, out), in...  46.9 us
    unnamed x10, local copies, waits for them, and re-layouts  11.4 us

profile of v1, /device:TPU:0, one launch (start us, length us, event | category | flops | bytes accessed | tf_op | source)
XLA Modules:
  0.0 61.1 jit_solution(13990082961551715652)
XLA Ops:
  0.6 0.7 %convert_element_type.4 = f32[16]{0:T(128)S(1)} convert(s32[16]{0:T(128)} %param.16) | non-fusion elementwise | flops 16 | bytes 128 | tf_op jit(solution)/shard_map/convert_element_type | solution.py:250
  1.3 0.7 %fusion.pick_ref = f32[16,16]{1,0:T(8,128)S(1)} fusion(f32[16]{0:T(128)S(1)} %convert_element_type.4, s32[16]{0:T(128)} %param.17), kind=kLoop, calls=%fused_computation.1 | loop fusion | flops 512 | bytes 1152 | tf_op jit(solution)/shard_map/jit(_where)/select_n | solution.py:248
  2.0 0.8 %copy.15.len_ref = s32[4,16,1]{2,1,0:T(8,128)S(1)} copy(s32[4,16,1]{1,0,2:T(4,128)} %bitcast.5) | data formatting | bytes 512 | tf_op jit(solution)/shard_map/broadcast_in_dim | solution.py:283
  2.8 1.1 %copy.11.res_hbm = f32[4,16,10,128]{3,2,1,0:T(8,128)S(1)} copy(f32[4,16,10,128]{3,1,2,0:T(8,128)} %param.9) | data formatting | bytes 655360 | tf_op args[0]
  3.9 1.3 %copy.13.wall_ref = f32[4,16,10,10]{3,2,1,0:T(8,128)S(1)} copy(f32[4,16,10,10]{1,0,3,2:T(4,128)} %param.11) | data formatting | bytes 51200 | tf_op args[2]
  5.1 2.2 %copy.14.off_ref = f32[4,4,16,10,10]{4,3,2,1,0:T(8,128)S(1)} copy(f32[4,4,16,10,10]{2,1,4,3,0:T(4,128)} %param.14) | data formatting | bytes 204800 | tf_op args[5]
  7.3 0.0 copy-start
  7.4 0.0 copy-start.1
  7.4 5.4 %copy.12.dinv_hbm = f32[4,16,10,10,128]{4,3,2,1,0:T(8,128)} copy(f32[4,16,10,10,128]{4,1,3,2,0:T(8,128)} %param.10) | data formatting | bytes 6553600 | tf_op args[1]
  12.7 0.0 copy-done
  12.7 0.0 copy-done.1
  12.7 46.9 %shard_map.104 = (f32[10,4,16,128]{3,2,1,0:T(8,128)S(1)}, f32[10,4,16,128]{3,2,1,0:T(8,128)S(1)}) custom-call(f32[4,16,10,128]{3,2,1,0:T(8,128)S(1)} %copy.11.res_hbm, f32[4,16,10,10,128]{4,3,2,1,0:T(8,128)} %copy.12.dinv_hbm, f32[4,16,10,10]{3,2,1,0:T(8,128)S(1)} %copy.13.wall_ref, f32[4,16,128]{2,1,0:T(8,128)S(1)} %copy-done, f32[4,16,128]{2,1,0:T(8,128)S(1)} %copy-done.1, ...), custom_call_target="tpu_custom_call" | custom-call | tf_op jit(solution)/shard_map/pallas_call | solution.py:255
  59.6 0.8 %copy.16 = f32[4,16,10,128]{3,1,2,0:T(8,128)} copy(f32[4,16,10,128]{3,1,0,2:T(8,128)S(1)} %bitcast.4) | data formatting | bytes 655360
  60.4 0.8 %copy.17 = f32[4,16,10,128]{3,1,2,0:T(8,128)} copy(f32[4,16,10,128]{3,1,0,2:T(8,128)S(1)} %bitcast.3) | data formatting | bytes 655360
Async XLA Ops:
  7.3 5.4 %copy-start = (f32[4,16,128]{2,1,0:T(8,128)S(1)}, f32[4,16,128]{2,1,0:T(8,128)}, u32[]{:S(2)}) copy-start(f32[4,16,128]{2,1,0:T(8,128)} %low_ref.1) | copy-start | bytes 98308
  7.4 5.4 %copy-start.1 = (f32[4,16,128]{2,1,0:T(8,128)S(1)}, f32[4,16,128]{2,1,0:T(8,128)}, u32[]{:S(2)}) copy-start(f32[4,16,128]{2,1,0:T(8,128)} %up_ref.1) | copy-start | bytes 98308

commit v2 on v1

v2 whole, which is shorter than its diff:
```python
import functools
import jax
import jax.numpy as jnp
from jax import lax
from jax.experimental import pallas as pl
from jax.experimental.pallas import tpu as pltpu
from jax.sharding import PartitionSpec as P

INNER = 4
SUB = 8
MESH = pl.DeviceIdType.MESH


def kernel(sizes, res, dinv_hbm, wall_ref, low_ref, up_ref, off_ref, len_ref, flag_ref, partner_ref,
           upd_ref, next_ref,
           dinv, jtab, flat, coef, rhs, lowm, upm, act, u, polar, left_out, right_out,
           left_in, right_in, load_sem, send_sem, recv_sem):
    n_sr, n_az, rows, lines, nv, points = sizes
    halves = lines // SUB
    groups = rows * halves
    sr, az = lax.axis_index("sr"), lax.axis_index("az")
    west, east = lax.rem(az + n_az - 1, n_az), lax.rem(az + 1, n_az)
    across = lax.rem(az + n_az // 2, n_az)
    last = n_sr - 1

    barrier = pltpu.get_barrier_semaphore()

    def greet(dst):
        pl.semaphore_signal(barrier, inc=1, device_id=dst, device_id_type=MESH)

    greet((sr, west))
    greet((sr, east))

    @pl.when(sr > 0)
    def _():
        greet((sr - 1, az))

    @pl.when(sr < last)
    def _():
        greet((sr + 1, az))

    @pl.when(sr == 0)
    def _():
        greet((0, across))

    def load(i):
        return pltpu.make_async_copy(dinv_hbm.at[i], dinv.at[i], load_sem.at[i])

    for i in range(rows):
        load(i).start()

    lane = lax.broadcasted_iota(jnp.int32, (SUB, points), 1)

    @pl.when(sr == last)
    def _():
        u[0, rows + 1] = jnp.zeros(u.shape[2:], jnp.float32)
        u[1, rows + 1] = jnp.zeros(u.shape[2:], jnp.float32)

    for i in range(rows):
        spot = slice(i * lines, (i + 1) * lines)
        for a in range(nv):
            entries = slice(a * nv, (a + 1) * nv)
            for d in range(4):
                flat[d, entries, spot] = off_ref[d, a, :, i, :]
            flat[4, entries, spot] = wall_ref[a, :, i, :]
        flat[4, nv * nv:nv * nv + 1, spot] = len_ref[i:i + 1, :].astype(jnp.float32)
    flat[4, nv * nv + 1:nv * nv + 2, 0:lines] = partner_ref[...].astype(jnp.float32)
    flat[4, nv * nv + 2:nv * nv + 3, 0:lines] = flag_ref[...].astype(jnp.float32)
    for d in range(5):
        coef[d] = jnp.transpose(flat[d])
    pick = jnp.where(
        coef[4, 0:lines, nv * nv + 1:nv * nv + 2]
        == lax.broadcasted_iota(jnp.int32, (lines, lines), 1).astype(jnp.float32),
        coef[4, 0:lines, nv * nv + 2:nv * nv + 3], 0.0)

    @pl.loop(0, groups)
    def _(g):
        i = lax.div(g, halves)
        eight = pl.ds(pl.multiple_of(lax.rem(g, halves) * SUB, SUB), SUB)
        lowm[g] = jnp.where(lane > 0, low_ref[i, eight, :], 0.0)
        upm[g] = jnp.where(lane < points - 1, up_ref[i, eight, :], 0.0)
        own = coef[4, pl.ds(pl.multiple_of(g * SUB, SUB), SUB), :]
        length = own[:, nv * nv:nv * nv + 1]
        act[g] = (lane.astype(jnp.float32) < length).astype(jnp.float32)
        for entry in range(nv * nv):
            jtab[g, entry] = jnp.broadcast_to(own[:, entry:entry + 1], (SUB, points))

    def inverse(i, half, vec):
        g = i * halves + half
        eight = slice(half * SUB, (half + 1) * SUB)
        out = [dinv[i, a, 0, eight, :] * vec[0] for a in range(nv)]
        for b in range(1, nv):
            for a in range(nv):
                out[a] = out[a] + dinv[i, a, b, eight, :] * vec[b]
        return [v * act[g] for v in out]

    def solve(slot, right_side):
        @pl.loop(0, rows)
        def _(i):
            if slot == 0:
                load(i).wait()

            def right(half):
                return [right_side[i, a, half * SUB:(half + 1) * SUB, :] for a in range(nv)]

            def step(_, xs):
                news = []
                for half in range(halves):
                    g = i * halves + half
                    x = xs[half]
                    below = [lowm[g] * pltpu.roll(v, 1, 1) for v in x]
                    above = [upm[g] * pltpu.roll(v, points - 1, 1) for v in x]
                    cross = right(half)
                    for b in range(nv):
                        for a in range(nv):
                            entry = jtab[g, a * nv + b]
                            cross[a] = cross[a] - entry * below[b]
                            cross[b] = cross[b] - entry * above[a]
                    news.append(tuple(inverse(i, half, cross)))
                return tuple(news)

            xs = tuple(tuple(inverse(i, half, right(half))) for half in range(halves))
            xs = lax.fori_loop(0, INNER, step, xs)
            for half in range(halves):
                base = SUB + half * SUB
                for a in range(nv):
                    u[slot, i + 1, a, base:base + SUB, :] = xs[half][a]
            for a in range(nv):
                left_out[slot, i, a] = xs[0][a][0]
                right_out[slot, i, a] = xs[halves - 1][a][SUB - 1]
            if slot == 1:
                for half in range(halves):
                    for a in range(nv):
                        upd_ref[i, a, half * SUB:(half + 1) * SUB, :] = xs[half][a]

    def exchange(slot):
        def copy(src, dst, kind, dev):
            return pltpu.make_async_remote_copy(
                src_ref=src, dst_ref=dst, send_sem=send_sem.at[slot, kind],
                recv_sem=recv_sem.at[slot, kind], device_id=dev, device_id_type=MESH)

        mid = pl.ds(SUB, lines)
        first, final = u.at[slot, 1, :, mid], u.at[slot, rows, :, mid]
        to_west = copy(left_out.at[slot], right_in.at[slot], 0, (sr, west))
        to_east = copy(right_out.at[slot], left_in.at[slot], 1, (sr, east))
        down = copy(first, u.at[slot, rows + 1, :, mid], 2, (jnp.maximum(sr - 1, 0), az))
        upward = copy(final, u.at[slot, 0, :, mid], 3, (jnp.minimum(sr + 1, last), az))
        over = copy(first, polar.at[slot], 4, (0, across))

        @pl.when(sr == 0)
        def _():
            over.start()

        @pl.when(sr > 0)
        def _():
            down.start()

        @pl.when(sr < last)
        def _():
            upward.start()

        to_west.start()
        to_east.start()

        to_west.wait()
        to_east.wait()
        for i in range(rows):
            for a in range(nv):
                u[slot, i + 1, a, SUB - 1] = left_in[slot, i, a]
                u[slot, i + 1, a, SUB + lines] = right_in[slot, i, a]

        @pl.when(sr > 0)
        def _():
            down.wait_send()
            upward.wait_recv()

        @pl.when(sr < last)
        def _():
            upward.wait_send()
            down.wait_recv()

        @pl.when(sr == 0)
        def _():
            over.wait()
            wide = jnp.concatenate([polar[slot, a] for a in range(nv)], axis=1)
            moved = jnp.dot(pick, wide, precision=lax.Precision.HIGHEST,
                            preferred_element_type=jnp.float32)
            for a in range(nv):
                u[slot, 0, a, mid] = moved[:, a * points:(a + 1) * points]

    def residual_less(slot, out):
        @pl.loop(0, rows)
        def _(i):
            for half in range(halves):
                g = i * halves + half
                base = SUB + half * SUB
                acc = [res[i, a, half * SUB:(half + 1) * SUB, :] for a in range(nv)]
                for d, (di, dk) in enumerate(((0, 0), (2, 0), (1, -1), (1, 1))):
                    near = [u[slot, i + di, b, base + dk:base + dk + SUB] for b in range(nv)]
                    own = coef[d, pl.ds(pl.multiple_of(g * SUB, SUB), SUB), :]
                    for b in range(nv):
                        for a in range(nv):
                            entry = own[:, a * nv + b:a * nv + b + 1]
                            acc[a] = acc[a] - jnp.broadcast_to(entry, (SUB, points)) * near[b]
                for a in range(nv):
                    out[i, a, half * SUB:(half + 1) * SUB, :] = acc[a]

    solve(0, res)

    @pl.when(sr == last)
    def _():
        pl.semaphore_wait(barrier, 3)

    @pl.when(sr < last)
    def _():
        pl.semaphore_wait(barrier, 4)

    exchange(0)
    residual_less(0, rhs)
    solve(1, rhs)
    exchange(1)
    residual_less(1, next_ref)


def body(mesh_sizes, residual, dinv, wall_jac, lower_coef, upper_coef, off_jac, lengths, axis_flag, partner):
    rows, lines, nv, points = residual.shape
    n_sr, n_az = mesh_sizes
    groups = rows * (lines // SUB)
    sizes = (n_sr, n_az, rows, lines, nv, points)
    vmem = pl.BlockSpec(memory_space=pltpu.VMEM)
    hbm = pl.BlockSpec(memory_space=pl.ANY)
    out = jax.ShapeDtypeStruct((rows, nv, lines, points), jnp.float32)
    f32 = jnp.float32
    update, next_rhs = pl.pallas_call(
        functools.partial(kernel, sizes),
        out_shape=(out, out),
        in_specs=[vmem, hbm] + [vmem] * 7,
        out_specs=(vmem, vmem),
        scratch_shapes=[
            pltpu.VMEM((rows, nv, nv, lines, points), f32),
            pltpu.VMEM((groups, nv * nv, SUB, points), f32),
            pltpu.VMEM((5, 128, 128), f32),
            pltpu.VMEM((5, 128, 128), f32),
            pltpu.VMEM((rows, nv, lines, points), f32),
            pltpu.VMEM((groups, SUB, points), f32),
            pltpu.VMEM((groups, SUB, points), f32),
            pltpu.VMEM((groups, SUB, points), f32),
            pltpu.VMEM((2, rows + 2, nv, lines + 2 * SUB, points), f32),
            pltpu.VMEM((2, nv, lines, points), f32),
            pltpu.VMEM((2, rows, nv, points), f32),
            pltpu.VMEM((2, rows, nv, points), f32),
            pltpu.VMEM((2, rows, nv, points), f32),
            pltpu.VMEM((2, rows, nv, points), f32),
            pltpu.SemaphoreType.DMA((rows,)),
            pltpu.SemaphoreType.DMA((2, 5)),
            pltpu.SemaphoreType.DMA((2, 5)),
        ],
        compiler_params=pltpu.CompilerParams(
            collective_id=0, has_side_effects=True, vmem_limit_bytes=48 * 2**20),
    )(residual.transpose(0, 2, 1, 3), dinv.transpose(0, 2, 3, 1, 4), wall_jac.transpose(2, 3, 0, 1),
      lower_coef, upper_coef, off_jac.transpose(0, 3, 4, 1, 2), lengths,
      axis_flag.reshape(1, lines), partner.reshape(1, lines))
    back = (0, 2, 1, 3)
    return update.transpose(back), next_rhs.transpose(back)


def solution(mesh):
    in_specs = (
        P("sr", "az", None, None),
        P("sr", "az", None, None, None),
        P("sr", "az", None, None),
        P("sr", "az", None),
        P("sr", "az", None),
        P(None, "sr", "az", None, None),
        P("sr", "az"),
        P("az"),
        P("az"),
    )
    out_specs = (P("sr", "az", None, None), P("sr", "az", None, None))
    sizes = (mesh.shape["sr"], mesh.shape["az"])
    return jax.shard_map(functools.partial(body, sizes), mesh=mesh, in_specs=in_specs,
                         out_specs=out_specs, check_vma=False)
```

time: 61.4 us -> 48.7 us (0.79)
  Pallas kernels: 46.9 us -> 37.7 us
  local copies, waits for them, and re-layouts: 12.2 us -> 9.92 us
  other arithmetic: 1.38 us -> 0 us
    pallas_call x1, Pallas kernels: 46.9 us -> 37.7 us  [body(): pl.pallas_call(functools.partial(kernel, sizes), out_shape=(out, out), in...]
    unnamed x10 -> x20, local copies, waits for them, and re-layouts: 11.4 us -> 9.92 us
    broadcast_in_dim x1 -> x0, local copies, waits for them, and re-layouts: 0.78 us -> none  [body(): lengths[:, :, None]]
    select_n x1 -> x0, other arithmetic: 0.73 us -> none  [body(): jnp.where(partner[:, None] == lax.broadcasted_iota(jnp.int32, (lines, lin...]
    convert_element_type x1 -> x0, other arithmetic: 0.66 us -> none  [body(): axis_flag[:, None].astype(jnp.float32)]
where the time goes in v2:
time: 48.7 us; the launch traced here: 48.2 us
  Pallas kernels  37.7 us (77%)
  local copies, waits for them, and re-layouts  9.92 us (20%)
  between operations  0.66 us (1%)
    pallas_call x1, Pallas kernels, body(): pl.pallas_call(functools.partial(kernel, sizes), out_shape=(out, out), in...  37.7 us
    unnamed x20, local copies, waits for them, and re-layouts  9.92 us

profile of v2, /device:TPU:0, one launch (start us, length us, event | category | flops | bytes accessed | tf_op | source)
XLA Modules:
  0.0 48.2 jit_solution(14506527239151752950)
XLA Ops:
  0.6 0.0 copy-start
  0.6 1.9 %copy-done = f32[4,16,10,10,128]{4,1,3,2,0:T(8,128)S(1)} copy-done((f32[4,16,10,10,128]{4,1,3,2,0:T(8,128)S(1)}, f32[4,16,10,10,128]{4,1,3,2,0:T(8,128)}, u32[]{:S(2)}) %copy-start) | copy-done | bytes 3276824
  2.6 0.0 copy-start.1
  2.6 1.1 %copy-done.1 = f32[4,4,16,10,10]{2,1,4,3,0:T(4,128)S(1)} copy-done((f32[4,4,16,10,10]{2,1,4,3,0:T(4,128)S(1)}, f32[4,4,16,10,10]{2,1,4,3,0:T(4,128)}, u32[]{:S(2)}) %copy-start.1) | copy-done | bytes 102424
  3.7 0.0 copy-start.2
  3.7 1.0 %copy-done.2 = f32[4,16,10,128]{3,1,2,0:T(8,128)S(1)} copy-done((f32[4,16,10,128]{3,1,2,0:T(8,128)S(1)}, f32[4,16,10,128]{3,1,2,0:T(8,128)}, u32[]{:S(2)}) %copy-start.2) | copy-done | bytes 327704
  4.7 0.0 copy-start.3
  4.7 0.9 %copy-done.3 = f32[4,16,10,10]{1,0,3,2:T(4,128)S(1)} copy-done((f32[4,16,10,10]{1,0,3,2:T(4,128)S(1)}, f32[4,16,10,10]{1,0,3,2:T(4,128)}, u32[]{:S(2)}) %copy-start.3) | copy-done | bytes 25624
  5.6 0.0 copy-start.4
  5.6 0.8 %copy-done.4 = f32[4,16,128]{2,1,0:T(8,128)S(1)} copy-done((f32[4,16,128]{2,1,0:T(8,128)S(1)}, f32[4,16,128]{2,1,0:T(8,128)}, u32[]{:S(2)}) %copy-start.4) | copy-done | bytes 32792
  6.4 0.0 copy-start.5
  6.4 0.8 %copy-done.5 = f32[4,16,128]{2,1,0:T(8,128)S(1)} copy-done((f32[4,16,128]{2,1,0:T(8,128)S(1)}, f32[4,16,128]{2,1,0:T(8,128)}, u32[]{:S(2)}) %copy-start.5) | copy-done | bytes 32792
  7.1 0.0 copy-start.6
  7.1 0.7 %copy-done.6 = s32[4,16]{1,0:T(4,128)S(1)} copy-done((s32[4,16]{1,0:T(4,128)S(1)}, s32[4,16]{1,0:T(4,128)}, u32[]{:S(2)}) %copy-start.6) | copy-done | bytes 280
  7.8 0.0 copy-start.7
  7.8 0.7 %copy-done.7 = s32[16]{0:T(128)S(1)} copy-done((s32[16]{0:T(128)S(1)}, s32[16]{0:T(128)}, u32[]{:S(2)}) %copy-start.7) | copy-done | bytes 88
  8.5 0.0 copy-start.8
  8.5 0.7 %copy-done.8 = s32[16]{0:T(128)S(1)} copy-done((s32[16]{0:T(128)S(1)}, s32[16]{0:T(128)}, u32[]{:S(2)}) %copy-start.8) | copy-done | bytes 88
  9.1 37.7 %shard_map.104 = (f32[4,10,16,128]{3,2,1,0:T(8,128)S(1)}, f32[4,10,16,128]{3,2,1,0:T(8,128)S(1)}) custom-call(f32[4,10,16,128]{3,2,1,0:T(8,128)S(1)} %bitcast.10, f32[4,10,10,16,128]{4,3,2,1,0:T(8,128)S(1)} %bitcast.8, f32[10,10,4,16]{3,2,1,0:T(4,128)S(1)} %bitcast.13, f32[4,16,128]{2,1,0:T(8,128)S(1)} %copy-done.4, f32[4,16,128]{2,1,0:T(8,128)S(1)} %copy-done.5, ...), custom_call_target="tpu_custom_call" | custom-call | tf_op jit(solution)/shard_map/pallas_call | solution.py:234
  46.8 0.7 %copy.13 = f32[4,16,10,128]{3,1,2,0:T(8,128)} copy(f32[4,16,10,128]{3,1,2,0:T(8,128)S(1)} %bitcast.12) | data formatting | bytes 655360
  47.5 0.7 %copy.14 = f32[4,16,10,128]{3,1,2,0:T(8,128)} copy(f32[4,16,10,128]{3,1,2,0:T(8,128)S(1)} %bitcast.11) | data formatting | bytes 655360
Async XLA Ops:
  0.6 1.9 %copy-start = (f32[4,16,10,10,128]{4,1,3,2,0:T(8,128)S(1)}, f32[4,16,10,10,128]{4,1,3,2,0:T(8,128)}, u32[]{:S(2)}) copy-start(f32[4,16,10,10,128]{4,1,3,2,0:T(8,128)} %param.10) | copy-start | bytes 9830404
  2.6 1.1 %copy-start.1 = (f32[4,4,16,10,10]{2,1,4,3,0:T(4,128)S(1)}, f32[4,4,16,10,10]{2,1,4,3,0:T(4,128)}, u32[]{:S(2)}) copy-start(f32[4,4,16,10,10]{2,1,4,3,0:T(4,128)} %param.14) | copy-start | bytes 307204
  3.7 1.0 %copy-start.2 = (f32[4,16,10,128]{3,1,2,0:T(8,128)S(1)}, f32[4,16,10,128]{3,1,2,0:T(8,128)}, u32[]{:S(2)}) copy-start(f32[4,16,10,128]{3,1,2,0:T(8,128)} %param.9) | copy-start | bytes 983044
  4.7 0.9 %copy-start.3 = (f32[4,16,10,10]{1,0,3,2:T(4,128)S(1)}, f32[4,16,10,10]{1,0,3,2:T(4,128)}, u32[]{:S(2)}) copy-start(f32[4,16,10,10]{1,0,3,2:T(4,128)} %param.11) | copy-start | bytes 76804
  5.6 0.8 %copy-start.4 = (f32[4,16,128]{2,1,0:T(8,128)S(1)}, f32[4,16,128]{2,1,0:T(8,128)}, u32[]{:S(2)}) copy-start(f32[4,16,128]{2,1,0:T(8,128)} %low_ref.1) | copy-start | bytes 98308
  6.4 0.8 %copy-start.5 = (f32[4,16,128]{2,1,0:T(8,128)S(1)}, f32[4,16,128]{2,1,0:T(8,128)}, u32[]{:S(2)}) copy-start(f32[4,16,128]{2,1,0:T(8,128)} %up_ref.1) | copy-start | bytes 98308
  7.1 0.7 %copy-start.6 = (s32[4,16]{1,0:T(4,128)S(1)}, s32[4,16]{1,0:T(4,128)}, u32[]{:S(2)}) copy-start(s32[4,16]{1,0:T(4,128)} %len_ref.1) | copy-start | bytes 772
  7.8 0.7 %copy-start.7 = (s32[16]{0:T(128)S(1)}, s32[16]{0:T(128)}, u32[]{:S(2)}) copy-start(s32[16]{0:T(128)} %param.16) | copy-start | bytes 196
  8.5 0.7 %copy-start.8 = (s32[16]{0:T(128)S(1)}, s32[16]{0:T(128)}, u32[]{:S(2)}) copy-start(s32[16]{0:T(128)} %param.17) | copy-start | bytes 196

commit v3 on v2

--- a/solution.py
+++ b/solution.py
@@ -11,10 +11,11 @@
 MESH = pl.DeviceIdType.MESH
 
 
-def kernel(sizes, res, dinv_hbm, wall_ref, low_ref, up_ref, off_ref, len_ref, flag_ref, partner_ref,
+def kernel(sizes, res_hbm, dinv_hbm, wall_hbm, low_hbm, up_hbm, off_hbm, len_hbm, flag_hbm, partner_hbm,
            upd_ref, next_ref,
-           dinv, jtab, flat, coef, rhs, lowm, upm, act, u, polar, left_out, right_out,
-           left_in, right_in, load_sem, send_sem, recv_sem):
+           dinv, jtab, flat, coef, wide_off, rhs, lowm, upm, act, u, polar, left_out, right_out,
+           left_in, right_in, res, wall_ref, low_ref, up_ref, off_ref, len_ref, flag_ref, partner_ref,
+           load_sem, send_sem, recv_sem):
     n_sr, n_az, rows, lines, nv, points = sizes
     halves = lines // SUB
     groups = rows * halves
@@ -46,6 +47,11 @@
     def load(i):
         return pltpu.make_async_copy(dinv_hbm.at[i], dinv.at[i], load_sem.at[i])
 
+    small = [pltpu.make_async_copy(src, dst, load_sem.at[rows + at]) for at, (src, dst) in enumerate((
+        (off_hbm, off_ref), (wall_hbm, wall_ref), (len_hbm, len_ref), (flag_hbm, flag_ref),
+        (partner_hbm, partner_ref), (low_hbm, low_ref), (up_hbm, up_ref), (res_hbm, res)))]
+    for copy in small:
+        copy.start()
     for i in range(rows):
         load(i).start()
 
@@ -55,23 +61,30 @@
     def _():
         u[0, rows + 1] = jnp.zeros(u.shape[2:], jnp.float32)
         u[1, rows + 1] = jnp.zeros(u.shape[2:], jnp.float32)
+
+    for copy in small:
+        copy.wait()
 
     for i in range(rows):
         spot = slice(i * lines, (i + 1) * lines)
         for a in range(nv):
             entries = slice(a * nv, (a + 1) * nv)
+            flat[entries, spot] = wall_ref[a, :, i, :]
+        flat[nv * nv:nv * nv + 1, spot] = len_ref[i:i + 1, :].astype(jnp.float32)
+    flat[nv * nv + 1:nv * nv + 2, 0:lines] = partner_ref[...].astype(jnp.float32)
+    flat[nv * nv + 2:nv * nv + 3, 0:lines] = flag_ref[...].astype(jnp.float32)
+    coef[...] = jnp.transpose(flat[...])
+    for i in range(rows):
+        for half in range(halves):
             for d in range(4):
-                flat[d, entries, spot] = off_ref[d, a, :, i, :]
-            flat[4, entries, spot] = wall_ref[a, :, i, :]
-        flat[4, nv * nv:nv * nv + 1, spot] = len_ref[i:i + 1, :].astype(jnp.float32)
-    flat[4, nv * nv + 1:nv * nv + 2, 0:lines] = partner_ref[...].astype(jnp.float32)
-    flat[4, nv * nv + 2:nv * nv + 3, 0:lines] = flag_ref[...].astype(jnp.float32)
-    for d in range(5):
-        coef[d] = jnp.transpose(flat[d])
+                for b in range(nv):
+                    at = (d * nv + b) * SUB
+                    wide_off[i * halves + half, :, at:at + SUB] = off_ref[
+                        d, :, b, i, half * SUB:(half + 1) * SUB]
     pick = jnp.where(
-        coef[4, 0:lines, nv * nv + 1:nv * nv + 2]
+        coef[0:lines, nv * nv + 1:nv * nv + 2]
         == lax.broadcasted_iota(jnp.int32, (lines, lines), 1).astype(jnp.float32),
-        coef[4, 0:lines, nv * nv + 2:nv * nv + 3], 0.0)
+        coef[0:lines, nv * nv + 2:nv * nv + 3], 0.0)
 
     @pl.loop(0, groups)
     def _(g):
@@ -79,7 +92,7 @@
         eight = pl.ds(pl.multiple_of(lax.rem(g, halves) * SUB, SUB), SUB)
         lowm[g] = jnp.where(lane > 0, low_ref[i, eight, :], 0.0)
         upm[g] = jnp.where(lane < points - 1, up_ref[i, eight, :], 0.0)
-        own = coef[4, pl.ds(pl.multiple_of(g * SUB, SUB), SUB), :]
+        own = coef[pl.ds(pl.multiple_of(g * SUB, SUB), SUB), :]
         length = own[:, nv * nv:nv * nv + 1]
         act[g] = (lane.astype(jnp.float32) < length).astype(jnp.float32)
         for entry in range(nv * nv):
@@ -103,11 +116,9 @@
             def right(half):
                 return [right_side[i, a, half * SUB:(half + 1) * SUB, :] for a in range(nv)]
 
-            def step(_, xs):
-                news = []
-                for half in range(halves):
+            def step(half, _, x):
+                if True:
                     g = i * halves + half
-                    x = xs[half]
                     below = [lowm[g] * pltpu.roll(v, 1, 1) for v in x]
                     above = [upm[g] * pltpu.roll(v, points - 1, 1) for v in x]
                     cross = right(half)
@@ -116,11 +127,12 @@
                             entry = jtab[g, a * nv + b]
                             cross[a] = cross[a] - entry * below[b]
                             cross[b] = cross[b] - entry * above[a]
-                    news.append(tuple(inverse(i, half, cross)))
-                return tuple(news)
-
-            xs = tuple(tuple(inverse(i, half, right(half))) for half in range(halves))
-            xs = lax.fori_loop(0, INNER, step, xs)
+                    return tuple(inverse(i, half, cross))
+
+            xs = []
+            for half in range(halves):
+                x = tuple(inverse(i, half, right(half)))
+                xs.append(lax.fori_loop(0, INNER, functools.partial(step, half), x, unroll=True))
             for half in range(halves):
                 base = SUB + half * SUB
                 for a in range(nv):
@@ -188,22 +200,25 @@
             for a in range(nv):
                 u[slot, 0, a, mid] = moved[:, a * points:(a + 1) * points]
 
+    span = 4 * nv * SUB
+    same_line = (lax.broadcasted_iota(jnp.int32, (SUB, span), 0)
+                 == lax.rem(lax.broadcasted_iota(jnp.int32, (SUB, span), 1), SUB))
+
     def residual_less(slot, out):
         @pl.loop(0, rows)
         def _(i):
             for half in range(halves):
                 g = i * halves + half
                 base = SUB + half * SUB
-                acc = [res[i, a, half * SUB:(half + 1) * SUB, :] for a in range(nv)]
-                for d, (di, dk) in enumerate(((0, 0), (2, 0), (1, -1), (1, 1))):
-                    near = [u[slot, i + di, b, base + dk:base + dk + SUB] for b in range(nv)]
-                    own = coef[d, pl.ds(pl.multiple_of(g * SUB, SUB), SUB), :]
-                    for b in range(nv):
-                        for a in range(nv):
-                            entry = own[:, a * nv + b:a * nv + b + 1]
-                            acc[a] = acc[a] - jnp.broadcast_to(entry, (SUB, points)) * near[b]
+                near = [u[slot, i + di, b, base + dk:base + dk + SUB]
+                        for di, dk in ((0, 0), (2, 0), (1, -1), (1, 1)) for b in range(nv)]
+                weights = [jnp.where(same_line, jnp.broadcast_to(wide_off[g, a:a + 1, :], (SUB, span)), 0.0)
+                           for a in range(nv)]
+                total = jnp.dot(jnp.concatenate(weights, axis=0), jnp.concatenate(near, axis=0),
+                                precision=lax.Precision.HIGHEST, preferred_element_type=jnp.float32)
                 for a in range(nv):
-                    out[i, a, half * SUB:(half + 1) * SUB, :] = acc[a]
+                    rows_at = slice(half * SUB, (half + 1) * SUB)
+                    out[i, a, rows_at, :] = res[i, a, rows_at, :] - total[a * SUB:(a + 1) * SUB]
 
     solve(0, res)
 
@@ -234,13 +249,14 @@
     update, next_rhs = pl.pallas_call(
         functools.partial(kernel, sizes),
         out_shape=(out, out),
-        in_specs=[vmem, hbm] + [vmem] * 7,
+        in_specs=[hbm] * 9,
         out_specs=(vmem, vmem),
         scratch_shapes=[
             pltpu.VMEM((rows, nv, nv, lines, points), f32),
             pltpu.VMEM((groups, nv * nv, SUB, points), f32),
-            pltpu.VMEM((5, 128, 128), f32),
-            pltpu.VMEM((5, 128, 128), f32),
+            pltpu.VMEM((128, 128), f32),
+            pltpu.VMEM((128, 128), f32),
+            pltpu.VMEM((groups, nv, 4 * nv * SUB), f32),
             pltpu.VMEM((rows, nv, lines, points), f32),
             pltpu.VMEM((groups, SUB, points), f32),
             pltpu.VMEM((groups, SUB, points), f32),
@@ -251,12 +267,20 @@
             pltpu.VMEM((2, rows, nv, points), f32),
             pltpu.VMEM((2, rows, nv, points), f32),
             pltpu.VMEM((2, rows, nv, points), f32),
-            pltpu.SemaphoreType.DMA((rows,)),
+            pltpu.VMEM((rows, nv, lines, points), f32),
+            pltpu.VMEM((nv, nv, rows, lines), f32),
+            pltpu.VMEM((rows, lines, points), f32),
+            pltpu.VMEM((rows, lines, points), f32),
+            pltpu.VMEM((4, nv, nv, rows, lines), f32),
+            pltpu.VMEM((rows, lines), jnp.int32),
+            pltpu.VMEM((1, lines), jnp.int32),
+            pltpu.VMEM((1, lines), jnp.int32),
+            pltpu.SemaphoreType.DMA((rows + 8,)),
             pltpu.SemaphoreType.DMA((2, 5)),
             pltpu.SemaphoreType.DMA((2, 5)),
         ],
         compiler_params=pltpu.CompilerParams(
-            collective_id=0, has_side_effects=True, vmem_limit_bytes=48 * 2**20),
+            collective_id=0, has_side_effects=True, vmem_limit_bytes=64 * 2**20),
     )(residual.transpose(0, 2, 1, 3), dinv.transpose(0, 2, 3, 1, 4), wall_jac.transpose(2, 3, 0, 1),
       lower_coef, upper_coef, off_jac.transpose(0, 3, 4, 1, 2), lengths,
       axis_flag.reshape(1, lines), partner.reshape(1, lines))

time: 48.7 us -> 33.4 us (0.69)
  Pallas kernels: 37.7 us -> 29.2 us
  local copies, waits for them, and re-layouts: 9.92 us -> 3.44 us
    pallas_call x1, Pallas kernels: 37.7 us -> 29.2 us  [body(): pl.pallas_call(functools.partial(kernel, sizes), out_shape=(out, out), in...]
    unnamed x20 -> x2, local copies, waits for them, and re-layouts: 9.92 us -> 3.44 us
where the time goes in v3:
time: 33.4 us; the launch traced here: 33.2 us
  Pallas kernels  29.2 us (87%)
  local copies, waits for them, and re-layouts  3.44 us (10%)
  between operations  0.64 us (2%)
    pallas_call x1, Pallas kernels, body(): pl.pallas_call(functools.partial(kernel, sizes), out_shape=(out, out), in...  29.2 us
    unnamed x2, local copies, waits for them, and re-layouts  3.44 us

profile of v3, /device:TPU:0, one launch (start us, length us, event | category | flops | bytes accessed | tf_op | source)
XLA Modules:
  0.0 33.2 jit_solution(13666809512372750912)
XLA Ops:
  0.6 29.2 %shard_map.104 = (f32[4,10,16,128]{3,2,1,0:T(8,128)}, f32[4,10,16,128]{3,2,1,0:T(8,128)}) custom-call(f32[4,10,16,128]{3,2,1,0:T(8,128)} %bitcast.10, f32[4,10,10,16,128]{4,3,2,1,0:T(8,128)} %bitcast.8, f32[10,10,4,16]{3,2,1,0:T(4,128)} %bitcast.13, f32[4,16,128]{2,1,0:T(8,128)} %low_hbm.1, f32[4,16,128]{2,1,0:T(8,128)} %up_hbm.1, ...), custom_call_target="tpu_custom_call" | custom-call | tf_op jit(solution)/shard_map/pallas_call | solution.py:249
  29.8 1.7 %copy.13 = f32[4,16,10,128]{3,1,2,0:T(8,128)} copy(f32[4,16,10,128]{3,1,2,0:T(8,128)} %bitcast.12) | data formatting | bytes 655360
  31.5 1.7 %copy.14 = f32[4,16,10,128]{3,1,2,0:T(8,128)} copy(f32[4,16,10,128]{3,1,2,0:T(8,128)} %bitcast.11) | data formatting | bytes 655360

commit v4 on v3

--- a/solution.py
+++ b/solution.py
@@ -52,8 +52,8 @@
         (partner_hbm, partner_ref), (low_hbm, low_ref), (up_hbm, up_ref), (res_hbm, res)))]
     for copy in small:
         copy.start()
-    for i in range(rows):
-        load(i).start()
+    for j in range(rows):
+        load(j * (rows - 1) % rows).start()
 
     lane = lax.broadcasted_iota(jnp.int32, (SUB, points), 1)
 
@@ -107,9 +107,76 @@
                 out[a] = out[a] + dinv[i, a, b, eight, :] * vec[b]
         return [v * act[g] for v in out]
 
+    mid = pl.ds(SUB, lines)
+
+    def copy(slot, src, dst, kind, dev):
+        return pltpu.make_async_remote_copy(
+            src_ref=src, dst_ref=dst, send_sem=send_sem.at[slot, kind],
+            recv_sem=recv_sem.at[slot, kind], device_id=dev, device_id_type=MESH)
+
+    def to_west(slot, i):
+        return copy(slot, left_out.at[slot, i], right_in.at[slot, i], 3 + i, (sr, west))
+
+    def to_east(slot, i):
+        return copy(slot, right_out.at[slot, i], left_in.at[slot, i], 3 + rows + i, (sr, east))
+
+    def down(slot):
+        return copy(slot, u.at[slot, 1, :, mid], u.at[slot, rows + 1, :, mid], 0,
+                    (jnp.maximum(sr - 1, 0), az))
+
+    def upward(slot):
+        return copy(slot, u.at[slot, rows, :, mid], u.at[slot, 0, :, mid], 1,
+                    (jnp.minimum(sr + 1, last), az))
+
+    def over(slot):
+        return copy(slot, u.at[slot, 1, :, mid], polar.at[slot], 2, (0, across))
+
+    def send(slot, i):
+        @pl.when(jnp.logical_and(i == 0, sr == 0))
+        def _():
+            over(slot).start()
+
+        @pl.when(jnp.logical_and(i == 0, sr > 0))
+        def _():
+            down(slot).start()
+
+        @pl.when(jnp.logical_and(i == rows - 1, sr < last))
+        def _():
+            upward(slot).start()
+
+        to_west(slot, i).start()
+        to_east(slot, i).start()
+
+    def receive(slot, i):
+        to_west(slot, i).wait()
+        to_east(slot, i).wait()
+        for a in range(nv):
+            u[slot, i + 1, a, SUB - 1] = left_in[slot, i, a]
+            u[slot, i + 1, a, SUB + lines] = right_in[slot, i, a]
+
+        @pl.when(jnp.logical_and(i == 0, sr > 0))
+        def _():
+            down(slot).wait_send()
+            upward(slot).wait_recv()
+
+        @pl.when(jnp.logical_and(i == rows - 1, sr < last))
+        def _():
+            upward(slot).wait_send()
+            down(slot).wait_recv()
+
+        @pl.when(jnp.logical_and(i == 0, sr == 0))
+        def _():
+            over(slot).wait()
+            wide = jnp.concatenate([polar[slot, a] for a in range(nv)], axis=1)
+            moved = jnp.dot(pick, wide, precision=lax.Precision.HIGHEST,
+                            preferred_element_type=jnp.float32)
+            for a in range(nv):
+                u[slot, 0, a, mid] = moved[:, a * points:(a + 1) * points]
+
     def solve(slot, right_side):
         @pl.loop(0, rows)
-        def _(i):
+        def _(j):
+            i = lax.rem(j * (rows - 1), rows)
             if slot == 0:
                 load(i).wait()
 
@@ -140,73 +207,21 @@
             for a in range(nv):
                 left_out[slot, i, a] = xs[0][a][0]
                 right_out[slot, i, a] = xs[halves - 1][a][SUB - 1]
+            send(slot, i)
             if slot == 1:
                 for half in range(halves):
                     for a in range(nv):
                         upd_ref[i, a, half * SUB:(half + 1) * SUB, :] = xs[half][a]
 
-    def exchange(slot):
-        def copy(src, dst, kind, dev):
-            return pltpu.make_async_remote_copy(
-                src_ref=src, dst_ref=dst, send_sem=send_sem.at[slot, kind],
-                recv_sem=recv_sem.at[slot, kind], device_id=dev, device_id_type=MESH)
-
-        mid = pl.ds(SUB, lines)
-        first, final = u.at[slot, 1, :, mid], u.at[slot, rows, :, mid]
-        to_west = copy(left_out.at[slot], right_in.at[slot], 0, (sr, west))
-        to_east = copy(right_out.at[slot], left_in.at[slot], 1, (sr, east))
-        down = copy(first, u.at[slot, rows + 1, :, mid], 2, (jnp.maximum(sr - 1, 0), az))
-        upward = copy(final, u.at[slot, 0, :, mid], 3, (jnp.minimum(sr + 1, last), az))
-        over = copy(first, polar.at[slot], 4, (0, across))
-
-        @pl.when(sr == 0)
-        def _():
-            over.start()
-
-        @pl.when(sr > 0)
-        def _():
-            down.start()
-
-        @pl.when(sr < last)
-        def _():
-            upward.start()
-
-        to_west.start()
-        to_east.start()
-
-        to_west.wait()
-        to_east.wait()
-        for i in range(rows):
-            for a in range(nv):
-                u[slot, i + 1, a, SUB - 1] = left_in[slot, i, a]
-                u[slot, i + 1, a, SUB + lines] = right_in[slot, i, a]
-
-        @pl.when(sr > 0)
-        def _():
-            down.wait_send()
-            upward.wait_recv()
-
-        @pl.when(sr < last)
-        def _():
-            upward.wait_send()
-            down.wait_recv()
-
-        @pl.when(sr == 0)
-        def _():
-            over.wait()
-            wide = jnp.concatenate([polar[slot, a] for a in range(nv)], axis=1)
-            moved = jnp.dot(pick, wide, precision=lax.Precision.HIGHEST,
-                            preferred_element_type=jnp.float32)
-            for a in range(nv):
-                u[slot, 0, a, mid] = moved[:, a * points:(a + 1) * points]
-
     span = 4 * nv * SUB
     same_line = (lax.broadcasted_iota(jnp.int32, (SUB, span), 0)
                  == lax.rem(lax.broadcasted_iota(jnp.int32, (SUB, span), 1), SUB))
 
     def residual_less(slot, out):
         @pl.loop(0, rows)
-        def _(i):
+        def _(j):
+            i = lax.rem(j * (rows - 1), rows)
+            receive(slot, i)
             for half in range(halves):
                 g = i * halves + half
                 base = SUB + half * SUB
@@ -220,20 +235,17 @@
                     rows_at = slice(half * SUB, (half + 1) * SUB)
                     out[i, a, rows_at, :] = res[i, a, rows_at, :] - total[a * SUB:(a + 1) * SUB]
 
+    @pl.when(sr == last)
+    def _():
+        pl.semaphore_wait(barrier, 3)
+
+    @pl.when(sr < last)
+    def _():
+        pl.semaphore_wait(barrier, 4)
+
     solve(0, res)
-
-    @pl.when(sr == last)
-    def _():
-        pl.semaphore_wait(barrier, 3)
-
-    @pl.when(sr < last)
-    def _():
-        pl.semaphore_wait(barrier, 4)
-
-    exchange(0)
     residual_less(0, rhs)
     solve(1, rhs)
-    exchange(1)
     residual_less(1, next_ref)
 
 
@@ -276,8 +288,8 @@
             pltpu.VMEM((1, lines), jnp.int32),
             pltpu.VMEM((1, lines), jnp.int32),
             pltpu.SemaphoreType.DMA((rows + 8,)),
-            pltpu.SemaphoreType.DMA((2, 5)),
-            pltpu.SemaphoreType.DMA((2, 5)),
+            pltpu.SemaphoreType.DMA((2, 3 + 2 * rows)),
+            pltpu.SemaphoreType.DMA((2, 3 + 2 * rows)),
         ],
         compiler_params=pltpu.CompilerParams(
             collective_id=0, has_side_effects=True, vmem_limit_bytes=64 * 2**20),

time: 33.4 us -> 28.4 us (0.85)
  Pallas kernels: 29.2 us -> 24.1 us
    pallas_call x1, Pallas kernels: 29.2 us -> 24.1 us  [body(): pl.pallas_call(functools.partial(kernel, sizes), out_shape=(out, out), in...]
where the time goes in v4:
time: 28.4 us; the launch traced here: 28.2 us
  Pallas kernels  24.1 us (85%)
  local copies, waits for them, and re-layouts  3.44 us (12%)
  between operations  0.64 us (2%)
    pallas_call x1, Pallas kernels, body(): pl.pallas_call(functools.partial(kernel, sizes), out_shape=(out, out), in...  24.1 us
    unnamed x2, local copies, waits for them, and re-layouts  3.44 us

profile of v4, /device:TPU:0, one launch (start us, length us, event | category | flops | bytes accessed | tf_op | source)
XLA Modules:
  0.0 28.2 jit_solution(15420136122083581629)
XLA Ops:
  0.6 24.1 %shard_map.104 = (f32[4,10,16,128]{3,2,1,0:T(8,128)}, f32[4,10,16,128]{3,2,1,0:T(8,128)}) custom-call(f32[4,10,16,128]{3,2,1,0:T(8,128)} %bitcast.10, f32[4,10,10,16,128]{4,3,2,1,0:T(8,128)} %bitcast.8, f32[10,10,4,16]{3,2,1,0:T(4,128)} %bitcast.13, f32[4,16,128]{2,1,0:T(8,128)} %low_hbm.1, f32[4,16,128]{2,1,0:T(8,128)} %up_hbm.1, ...), custom_call_target="tpu_custom_call" | custom-call | tf_op jit(solution)/shard_map/pallas_call | solution.py:261
  24.8 1.7 %copy.13 = f32[4,16,10,128]{3,1,2,0:T(8,128)} copy(f32[4,16,10,128]{3,1,2,0:T(8,128)} %bitcast.12) | data formatting | bytes 655360
  26.5 1.7 %copy.14 = f32[4,16,10,128]{3,1,2,0:T(8,128)} copy(f32[4,16,10,128]{3,1,2,0:T(8,128)} %bitcast.11) | data formatting | bytes 655360

commit v5 on v4

--- a/solution.py
+++ b/solution.py
@@ -62,7 +62,7 @@
         u[0, rows + 1] = jnp.zeros(u.shape[2:], jnp.float32)
         u[1, rows + 1] = jnp.zeros(u.shape[2:], jnp.float32)
 
-    for copy in small:
+    for copy in small[1:]:
         copy.wait()
 
     for i in range(rows):
@@ -74,13 +74,6 @@
     flat[nv * nv + 1:nv * nv + 2, 0:lines] = partner_ref[...].astype(jnp.float32)
     flat[nv * nv + 2:nv * nv + 3, 0:lines] = flag_ref[...].astype(jnp.float32)
     coef[...] = jnp.transpose(flat[...])
-    for i in range(rows):
-        for half in range(halves):
-            for d in range(4):
-                for b in range(nv):
-                    at = (d * nv + b) * SUB
-                    wide_off[i * halves + half, :, at:at + SUB] = off_ref[
-                        d, :, b, i, half * SUB:(half + 1) * SUB]
     pick = jnp.where(
         coef[0:lines, nv * nv + 1:nv * nv + 2]
         == lax.broadcasted_iota(jnp.int32, (lines, lines), 1).astype(jnp.float32),
@@ -244,6 +237,14 @@
         pl.semaphore_wait(barrier, 4)
 
     solve(0, res)
+    small[0].wait()
+    for i in range(rows):
+        for half in range(halves):
+            for d in range(4):
+                for b in range(nv):
+                    at = (d * nv + b) * SUB
+                    wide_off[i * halves + half, :, at:at + SUB] = off_ref[
+                        d, :, b, i, half * SUB:(half + 1) * SUB]
     residual_less(0, rhs)
     solve(1, rhs)
     residual_less(1, next_ref)

time: 28.4 us -> 27.6 us (0.972)
  Pallas kernels: 24.1 us -> 23.3 us
    pallas_call x1, Pallas kernels: 24.1 us -> 23.3 us  [body(): pl.pallas_call(functools.partial(kernel, sizes), out_shape=(out, out), in...]
where the time goes in v5:
time: 27.6 us; the launch traced here: 27.4 us
  Pallas kernels  23.3 us (84%)
  local copies, waits for them, and re-layouts  3.44 us (12%)
  between operations  0.64 us (2%)
    pallas_call x1, Pallas kernels, body(): pl.pallas_call(functools.partial(kernel, sizes), out_shape=(out, out), in...  23.3 us
    unnamed x2, local copies, waits for them, and re-layouts  3.44 us

profile of v5, /device:TPU:0, one launch (start us, length us, event | category | flops | bytes accessed | tf_op | source)
XLA Modules:
  0.0 27.4 jit_solution(7580981127212053102)
XLA Ops:
  0.6 23.3 %shard_map.104 = (f32[4,10,16,128]{3,2,1,0:T(8,128)}, f32[4,10,16,128]{3,2,1,0:T(8,128)}) custom-call(f32[4,10,16,128]{3,2,1,0:T(8,128)} %bitcast.10, f32[4,10,10,16,128]{4,3,2,1,0:T(8,128)} %bitcast.8, f32[10,10,4,16]{3,2,1,0:T(4,128)} %bitcast.13, f32[4,16,128]{2,1,0:T(8,128)} %low_hbm.1, f32[4,16,128]{2,1,0:T(8,128)} %up_hbm.1, ...), custom_call_target="tpu_custom_call" | custom-call | tf_op jit(solution)/shard_map/pallas_call | solution.py:262
  24.0 1.7 %copy.13 = f32[4,16,10,128]{3,1,2,0:T(8,128)} copy(f32[4,16,10,128]{3,1,2,0:T(8,128)} %bitcast.12) | data formatting | bytes 655360
  25.7 1.7 %copy.14 = f32[4,16,10,128]{3,1,2,0:T(8,128)} copy(f32[4,16,10,128]{3,1,2,0:T(8,128)} %bitcast.11) | data formatting | bytes 655360
